TPU v7x, 512 devices: a whole 4x8x8 slice. The times are simulated.
512 devices in a mesh: row: 16 (over z, y_lo), col: 32 (over y_hi, x, core).
Axes of the slice: x: 4, y: 8 (y_hi: 4, y_lo: 2; y = y_hi * 2 + y_lo), z: 8, core: 2. Of those that a mesh axis runs over, the one named last changes fastest.
Arguments:
- pair: bfloat16 [768, 768, 128], P('row', 'col'), may hold values from -100 to 100
- ln_gain: float32 [128], replicated, may hold values from 0.1 to 1.9
- w_query: bfloat16 [128, 128], replicated, may hold values from -0.5 to 0.5
- w_keyval: bfloat16 [128, 256], replicated, may hold values from -0.5 to 0.5
- w_gate: bfloat16 [128, 128], replicated, may hold values from -0.5 to 0.5
- w_bias: bfloat16 [128, 4], replicated, may hold values from -16 to 16
- w_out: bfloat16 [128, 128], replicated, may hold values from -0.5 to 0.5
Outputs:
- update: bfloat16 [128, 768, 128], P('row', 'col')
All inputs are finite; a program needn't handle non-finite values.
Results may differ from a plain program's by a relative error of at most 0.0025.
The roundings to bfloat16 on the way count: a program that leaves them out, or rounds other values in their place, can miss the bound.
Values may be sent and summed in bfloat16 or wider, within the bound.
No kernel may reach another device: no remote copies, remote signals or barrier semaphores. Data moves between devices by JAX's collectives and lax.ppermute only.
A program may use at most 64 MiB of HBM per device.

v0:
```python
import jax
import jax.numpy as jnp
from jax import lax
from jax.experimental import pallas as pl
from jax.experimental.pallas import tpu as pltpu
from jax.sharding import PartitionSpec as P

QROWS = 8
KB = 24
HEADS = 4
LANES = 128
NROW = 16
N_RES = 768
NCOL = 32
F32 = jnp.float32
BF16 = jnp.bfloat16
VM = pltpu.VMEM


def whole(space=VM):
    return pl.BlockSpec(memory_space=space)


MASKS = (0, 1, 3, 2)


def norm_rows(block, gain):
    values = block.astype(F32)
    mean = jnp.mean(values, axis=-1, keepdims=True)
    centred = values - mean
    variance = jnp.mean(centred * centred, axis=-1, keepdims=True)
    return (centred * lax.rsqrt(variance + 1e-05) * gain).astype(BF16)


CHUNKS = ((0, 192), (192, 576), (576, 1152))


def front_kernel(
    rows_ref, gain_ref, wb_ref, nq_ref, tile_ref, held_ref, gain_vm, wb_vm, sems
):
    copies = []
    for i, (begin, end) in enumerate(CHUNKS):
        part = pl.ds(begin, end - begin)
        copies.append(pltpu.make_async_copy(rows_ref.at[part], held_ref.at[part], sems.at[i]))
    gain_copy = pltpu.make_async_copy(gain_ref, gain_vm, sems.at[3])
    wb_copy = pltpu.make_async_copy(wb_ref, wb_vm, sems.at[4])
    copies[0].start()
    gain_copy.start()
    wb_copy.start()
    copies[1].start()
    copies[2].start()
    lane = lax.broadcasted_iota(jnp.int32, (KB, LANES), 1)
    place = jnp.where(lane < HEADS * KB, lax.rem(lane, KB), -1)
    gain_copy.wait()
    gain = gain_vm[...]
    wb_copy.wait()
    wb = wb_vm[...].astype(F32)
    spread_t = [jnp.broadcast_to(wb[h : h + 1, :], (KB, LANES)) for h in range(HEADS)]
    spread_t.append(jnp.zeros((LANES - HEADS * KB, LANES), F32))
    spread_t = jnp.concatenate(spread_t, axis=0).astype(BF16)
    total = jnp.zeros((KB, LANES), F32)
    for i, (begin, end) in enumerate(CHUNKS):
        copies[i].wait()
        normed = norm_rows(held_ref[begin:end, :], gain)
        if i == 0:
            nq_ref[...] = normed
        wide = nt_dot(normed, spread_t)
        for j in range(begin // KB, end // KB):
            row = j * KB - begin
            total = jnp.where(place == j % KB, wide[row : row + KB, :], total)
            if j % KB == KB - 1:
                tile_ref[j + 1 - KB : j + 1, :] = total


def copies_kernel(tile_ref, out_ref, sems):
    sends = []
    for r in range(NROW):
        send = pltpu.make_async_copy(tile_ref, out_ref.at[r], sems.at[r])
        send.start()
        sends.append(send)
    for send in sends:
        send.wait()


def relay_kernel(own_ref, first_ref, second_ref, third_ref, out_ref):
    for a in range(QROWS):
        span = slice(a * KB, (a + 1) * KB)
        refs = (own_ref, first_ref, second_ref, third_ref)
        parts = [ref[span, :].astype(F32) for ref in refs]
        out_ref[a * 96 : (a + 1) * 96, :] = jnp.concatenate(parts, axis=0).astype(BF16)


HALF_K = NROW * KB


def join_kernel(third_ref, bias_ref, payload_ref, order_ref):
    rows = third_ref.shape[0]
    payload_ref[0:rows, :] = third_ref[...]
    col = lax.axis_index("col")
    core = lax.rem(col, 2)
    x = lax.rem(col // 2, 4)
    y_hi = col // 8
    place = 0
    rest = []
    for mask in MASKS:
        for y_mask in MASKS:
            slot = lax.bitwise_xor(y_hi, y_mask) * 4 + lax.bitwise_xor(x, mask)
            mine = pl.multiple_of((slot * 2 + core) * KB, 8)
            theirs = pl.multiple_of((slot * 2 + 1 - core) * KB, 8)
            order_ref[place : place + KB, :] = bias_ref[pl.ds(mine, KB), :]
            rest.append(bias_ref[pl.ds(theirs, KB), :])
            place += KB
    rest = jnp.concatenate(rest, axis=0)
    for term in range(3):
        part = rest.astype(BF16)
        rest = rest - part.astype(F32)
        begin = rows + term * HALF_K
        payload_ref[begin : begin + HALF_K, :] = part


def nt_dot(left, right):
    return lax.dot_general(left, right, (((1,), (1,)), ((), ())), preferred_element_type=F32)


def twice(block):
    zero = jnp.zeros_like(block)
    top = jnp.concatenate([block, zero], axis=1)
    return jnp.concatenate([top, jnp.concatenate([zero, block], axis=1)], axis=0)


def attend_kernel(
    own_ref, first_ref, second_ref, third_ref, theirs_a_ref, theirs_b_ref, order_ref,
    nq_ref, wq_ref, wkv_ref, wg_ref, wo_ref,
    out_ref, bias_ref, held_ref, gate_ref, gated_ref,
):
    sources = (
        own_ref, first_ref, second_ref, third_ref,
        theirs_a_ref.at[0], theirs_a_ref.at[1], theirs_a_ref.at[2], theirs_b_ref,
    )
    bias_ref[0:HALF_K, :] = order_ref[...]
    terms = []
    for term in range(3):
        begin = third_ref.shape[0] + term * HALF_K
        terms.append(theirs_b_ref[begin : begin + HALF_K, :].astype(F32))
    bias_ref[HALF_K:, :] = (terms[0] + terms[1]) + terms[2]
    nq = nq_ref[...]
    query = jnp.dot(nq, wq_ref[...], preferred_element_type=F32) * (1.0 / 32**0.5)
    query = query.astype(BF16).astype(F32)
    gate_ref[...] = jax.nn.sigmoid(jnp.dot(nq, wg_ref[...], preferred_element_type=F32))
    wk = twice(wkv_ref[:, :LANES].astype(F32)).astype(BF16)
    wvt = twice(wkv_ref[:, LANES:].astype(F32).T).astype(BF16)
    lane = lax.broadcasted_iota(jnp.int32, (KB, LANES), 1)
    zero = jnp.zeros((LANES, LANES), F32)
    for i in range(QROWS // 2):
        sides = []
        masked = []
        for a in (2 * i, 2 * i + 1):
            sides.append(
                jnp.concatenate([ref[a * 96 : (a + 1) * 96, :] for ref in sources], axis=0)
            )
            q = query[a * KB : (a + 1) * KB, :]
            parts = [jnp.where(lane // 32 == h, q, 0.0) for h in range(HEADS)]
            parts.append(jnp.zeros((LANES - HEADS * KB, LANES), F32))
            masked.append(jnp.concatenate(parts, axis=0))
        queries = jnp.concatenate(
            [
                jnp.concatenate([masked[0], zero], axis=1),
                jnp.concatenate([zero, masked[1]], axis=1),
            ],
            axis=0,
        ).astype(BF16)
        rows = jnp.concatenate(sides, axis=1)
        keys = jnp.dot(rows, wk, preferred_element_type=F32).astype(BF16)
        values_t = nt_dot(wvt, rows).astype(BF16)
        score = nt_dot(keys, queries)
        for n in range(2):
            a = 2 * i + n
            full = score[:, n * LANES : (n + 1) * LANES] + bias_ref[...]
            held_ref[a % 4] = full
            top = jnp.max(full, axis=0, keepdims=True)
            weights = jnp.exp(held_ref[a % 4] - top)
            total = jnp.sum(weights, axis=0, keepdims=True)
            high = weights.astype(BF16)
            low = (weights - high.astype(F32)).astype(BF16)
            both = jnp.dot(
                values_t[n * LANES : (n + 1) * LANES, :],
                jnp.concatenate([high, low], axis=1),
                preferred_element_type=F32,
            )
            attended = ((both[:, :LANES] + both[:, LANES:]) / total).T
            mine = jnp.zeros((KB, LANES), F32)
            for h in range(HEADS):
                mine = jnp.where(lane // 32 == h, attended[h * KB : (h + 1) * KB, :], mine)
            span = slice(a * KB, (a + 1) * KB)
            gated_ref[span, :] = gate_ref[span, :] * mine
    out_ref[...] = jnp.dot(
        gated_ref[...].astype(BF16), wo_ref[...], preferred_element_type=F32
    ).astype(BF16)


def permute_col(value, target):
    return lax.ppermute(value, "col", [(c, target(c)) for c in range(NCOL)])


def permute_all(value, target):
    pairs = []
    for r in range(NROW):
        for c in range(NCOL):
            r2, c2 = target(r, c)
            pairs.append((r * NCOL + c, r2 * NCOL + c2))
    return lax.ppermute(value, ("row", "col"), pairs)


def near_y(mask):
    return lambda c: c ^ (mask * 8)


def near_x(mask):
    return lambda c: c ^ (mask * 2)


def body(pair, ln_gain, w_query, w_keyval, w_gate, w_bias, w_out):
    shape = jax.ShapeDtypeStruct
    rows = pair.reshape(-1, LANES)
    nrows = QROWS * KB
    nq, tile = pl.pallas_call(
        front_kernel,
        in_specs=[whole(pl.ANY)] * 3,
        out_specs=[whole(), whole()],
        out_shape=[shape((nrows, LANES), BF16), shape((2 * KB, LANES), F32)],
        scratch_shapes=[
            VM(rows.shape, BF16),
            VM((1, LANES), F32),
            VM((HEADS, LANES), BF16),
            pltpu.SemaphoreType.DMA((5,)),
        ],
        name="front",
    )(rows, ln_gain.reshape(1, LANES), w_bias.T)
    ys = [nq] + [permute_col(nq, near_y(mask)) for mask in MASKS[1:]]
    tile = permute_all(tile, lambda r, c: (c // 2, 2 * r + c % 2))
    small = pltpu.CompilerParams(vmem_limit_bytes=16 * 1024 * 1024)
    tiles = pl.pallas_call(
        copies_kernel,
        in_specs=[whole()],
        out_specs=whole(pl.ANY),
        out_shape=shape((NROW, 2 * KB, LANES), F32),
        scratch_shapes=[pltpu.SemaphoreType.DMA((NROW,))],
        compiler_params=small,
        cost_estimate=pl.CostEstimate(flops=20 * 10**9, bytes_accessed=0, transcendentals=0),
        name="copies",
    )(tile)
    bias = lax.all_to_all(tiles, "row", 0, 0)
    piece = pl.pallas_call(
        relay_kernel,
        in_specs=[whole()] * 4,
        out_specs=whole(),
        out_shape=shape((4 * nrows, LANES), BF16),
        compiler_params=small,
        cost_estimate=pl.CostEstimate(flops=30 * 10**9, bytes_accessed=0, transcendentals=0),
        name="relay",
    )(*ys)
    first = permute_col(piece, near_x(1))
    second = permute_col(piece, near_x(3))
    third = permute_col(first, near_x(3))
    mine = [piece, first, second, third]
    last, order = pl.pallas_call(
        join_kernel,
        in_specs=[whole()] * 2,
        out_specs=[whole()] * 2,
        out_shape=[
            shape((4 * nrows + 3 * HALF_K, LANES), BF16),
            shape((HALF_K, LANES), F32),
        ],
        compiler_params=small,
        name="join",
    )(third, bias.reshape(-1, LANES))
    theirs = [permute_col(value, lambda c: c ^ 1) for value in (jnp.stack(mine[:3]), last)]
    out = pl.pallas_call(
        attend_kernel,
        in_specs=[whole()] * 12,
        out_specs=whole(),
        out_shape=shape((nrows, LANES), BF16),
        scratch_shapes=[
            VM((N_RES, LANES), F32),
            VM((4, 768, LANES), F32),
            VM((nrows, LANES), F32),
            VM((nrows, LANES), F32),
        ],
        compiler_params=pltpu.CompilerParams(vmem_limit_bytes=32 * 1024 * 1024),
        name="attend",
    )(*mine, *theirs, order, nq, w_query, w_keyval, w_gate, w_out)
    return out.reshape(QROWS, KB, LANES)


def solution(mesh):
    placed = (P("row", "col", None), P(), P(), P(), P(), P(), P())
    return jax.shard_map(
        body, mesh=mesh, in_specs=placed, out_specs=P("row", "col", None), check_vma=False
    )
```

profile of v0, /device:TPU:1, one launch (start us, length us, event | category | flops | bytes accessed | tf_op | source)
XLA Modules:
  0.0 60.4 jit_solution(18021350995892497360)
XLA Ops:
  0.0 2.5 %front.1 = (bf16[192,128]{1,0:T(8,128)(2,1)}, f32[48,128]{1,0:T(8,128)}) custom-call(bf16[1152,128]{1,0:T(8,128)(2,1)} %bitcast.12, f32[1,128]{1,0:T(1,128)} %bitcast.14, bf16[4,128]{1,0:T(4,128)(2,1)} %bitcast.13), custom_call_target="tpu_custom_call" | custom-call | tf_op jit(solution)/shard_map/front/pallas_call | solution.py:226
  2.5 1.4 %collective-permute-start.7 = (f32[48,128]{1,0:T(8,128)}, f32[48,128]{1,0:T(8,128)S(1)}, u32[]{:S(2)}, u32[]{:S(2)}) collective-permute-start(f32[48,128]{1,0:T(8,128)} %get-tuple-element.10), channel_id=1, source_target_pairs={{0,0},{1,1},{2,32},{3,33},{4,64},{5,65},{6,96},{7,97},{8,128},{9,1... | collective-permute-start | bytes 73736 | tf_op jit(solution)/shard_map/ppermute | solution.py:211
  3.9 9.2 %collective-permute-start = (bf16[192,128]{1,0:T(8,128)(2,1)}, bf16[192,128]{1,0:T(8,128)(2,1)S(1)}, u32[]{:S(2)}, u32[]{:S(2)}) collective-permute-start(bf16[192,128]{1,0:T(8,128)(2,1)} %get-tuple-element.9.own_ref.nq_ref), channel_id=1, source_target_pairs={{0,8},{1,9},{2,10},{3,11},{4,12},{5,13},{6,14},{7,15},{8,0},{9,1},... | collective-permute-start | bytes 147464 | tf_op jit(solution)/shard_map/ppermute | solution.py:202
  13.2 10.0 %collective-permute-start.1 = (bf16[192,128]{1,0:T(8,128)(2,1)}, bf16[192,128]{1,0:T(8,128)(2,1)S(1)}, u32[]{:S(2)}, u32[]{:S(2)}) collective-permute-start(bf16[192,128]{1,0:T(8,128)(2,1)} %get-tuple-element.9.own_ref.nq_ref), channel_id=1, source_target_pairs={{0,24},{1,25},{2,26},{3,27},{4,28},{5,29},{6,30},{7,31},{8,16},{9,... | collective-permute-start | bytes 147464 | tf_op jit(solution)/shard_map/ppermute | solution.py:202
  23.2 1.9 %collective-permute-start.2 = (bf16[192,128]{1,0:T(8,128)(2,1)}, bf16[192,128]{1,0:T(8,128)(2,1)S(1)}, u32[]{:S(2)}, u32[]{:S(2)}) collective-permute-start(bf16[192,128]{1,0:T(8,128)(2,1)} %get-tuple-element.9.own_ref.nq_ref), channel_id=1, source_target_pairs={{0,16},{1,17},{2,18},{3,19},{4,20},{5,21},{6,22},{7,23},{8,24},{9,... | collective-permute-start | bytes 147464 | tf_op jit(solution)/shard_map/ppermute | solution.py:202
  25.1 0.0 collective-permute-done.7.tile_ref
  25.1 0.9 %copies.1 = f32[16,48,128]{2,1,0:T(8,128)} custom-call(f32[48,128]{1,0:T(8,128)S(1)} %collective-permute-done.7.tile_ref), custom_call_target="tpu_custom_call" | custom-call | flops 20000000000 | tf_op jit(solution)/shard_map/copies/pallas_call | solution.py:242
  26.1 0.0 copy-start.1
  26.1 8.1 %all-to-all-start = ((f32[16,48,128]{2,1,0:T(8,128)}), f32[16,48,128]{2,1,0:T(8,128)S(1)}, u32[]{:S(2)}, u32[]{:S(2)}) async-start(f32[16,48,128]{2,1,0:T(8,128)} %copies.1), calls=%async_computation | async-start | bytes 786432 | tf_op jit(solution)/shard_map/all_to_all | solution.py:252
  34.2 3.2 %collective-permute-start.3 = (bf16[768,128]{1,0:T(8,128)(2,1)S(1)}, bf16[768,128]{1,0:T(8,128)(2,1)S(1)}, u32[]{:S(2)}, u32[]{:S(2)}) collective-permute-start(bf16[768,128]{1,0:T(8,128)(2,1)S(1)} %relay.1.own_ref), channel_id=1, source_target_pairs={{0,2},{1,3},{2,0},{3,1},{4,6},{5,7},{6,4},{7,5},{8,10},{9,11},{10,... | collective-permute-start | bytes 589832 | tf_op jit(solution)/shard_map/ppermute | solution.py:202
  37.5 3.2 %collective-permute-start.4 = (bf16[768,128]{1,0:T(8,128)(2,1)S(1)}, bf16[768,128]{1,0:T(8,128)(2,1)S(1)}, u32[]{:S(2)}, u32[]{:S(2)}) collective-permute-start(bf16[768,128]{1,0:T(8,128)(2,1)S(1)} %relay.1.own_ref), channel_id=1, source_target_pairs={{0,6},{1,7},{2,4},{3,5},{4,2},{5,3},{6,0},{7,1},{8,14},{9,15},{10,... | collective-permute-start | bytes 589832 | tf_op jit(solution)/shard_map/ppermute | solution.py:202
  40.7 0.3 collective-permute-done.3.first_ref
  41.0 4.0 %collective-permute-start.5 = (bf16[768,128]{1,0:T(8,128)(2,1)S(1)}, bf16[768,128]{1,0:T(8,128)(2,1)S(1)}, u32[]{:S(2)}, u32[]{:S(2)}) collective-permute-start(bf16[768,128]{1,0:T(8,128)(2,1)S(1)} %collective-permute-done.3.first_ref), channel_id=1, source_target_pairs={{0,6},{1,7},{2,4},{3,5},{4,2},{5,3},{6,0},{7,1},{8,14},{9,15},{10,... | collective-permute-start | bytes 589832 | tf_op jit(solution)/shard_map/ppermute | solution.py:202
  45.0 0.4 collective-permute-done.4.second_ref
  45.4 0.1 pad_maximum_fusion
  45.5 6.0 %collective-permute-start.6 = (bf16[3,768,128]{2,1,0:T(8,128)(2,1)S(1)}, bf16[3,768,128]{2,1,0:T(8,128)(2,1)S(1)}, u32[]{:S(2)}, u32[]{:S(2)}) collective-permute-start(bf16[3,768,128]{2,1,0:T(8,128)(2,1)S(1)} %pad_maximum_fusion), channel_id=1, source_target_pairs={{0,1},{1,0},{2,3},{3,2},{4,5},{5,4},{6,7},{7,6},{8,9},{9,8},{10,11... | collective-permute-start | bytes 1769480 | tf_op jit(solution)/shard_map/ppermute | solution.py:202
  51.5 0.0 copy-start
  51.6 0.0 copy-start.2
  51.6 0.0 copy-start.3
  51.6 0.0 copy-start.4
  51.6 0.1 join.1
  51.7 2.9 %collective-permute-start.8 = (bf16[1920,128]{1,0:T(8,128)(2,1)S(1)}, bf16[1920,128]{1,0:T(8,128)(2,1)S(1)}, u32[]{:S(2)}, u32[]{:S(2)}) collective-permute-start(bf16[1920,128]{1,0:T(8,128)(2,1)S(1)} %get-tuple-element.11), channel_id=1, source_target_pairs={{0,1},{1,0},{2,3},{3,2},{4,5},{5,4},{6,7},{7,6},{8,9},{9,8},{10,11... | collective-permute-start | bytes 1474568 | tf_op jit(solution)/shard_map/ppermute | solution.py:202
  54.6 1.5 %collective-permute-done.8.theirs_b_ref = bf16[1920,128]{1,0:T(8,128)(2,1)S(1)} collective-permute-done((bf16[1920,128]{1,0:T(8,128)(2,1)S(1)}, bf16[1920,128]{1,0:T(8,128)(2,1)S(1)}, u32[]{:S(2)}, u32[]{:S(2)}) %collective-permute-start.8) | collective-permute-done | bytes 491552 | tf_op jit(solution)/shard_map/ppermute | solution.py:202
  56.1 4.3 %attend.1 = bf16[192,128]{1,0:T(8,128)(2,1)} custom-call(bf16[768,128]{1,0:T(8,128)(2,1)S(1)} %relay.1.own_ref, bf16[768,128]{1,0:T(8,128)(2,1)S(1)} %collective-permute-done.3.first_ref, bf16[768,128]{1,0:T(8,128)(2,1)S(1)} %collective-permute-done.4.second_ref, bf16[768,128]{1,0:T(8,128)(2,1)S(1)} %collective-permute-done.5.third_ref, ...), custom_call_target="tpu_custom_call" | custom-call | tf_op jit(solution)/shard_map/attend/pallas_call | solution.py:278
  (12 shorter events, 0.1 us)
Async XLA Ops:
  2.5 22.6 %collective-permute-start.7 = (f32[48,128]{1,0:T(8,128)}, f32[48,128]{1,0:T(8,128)S(1)}, u32[]{:S(2)}, u32[]{:S(2)}) collective-permute-start(f32[48,128]{1,0:T(8,128)} %get-tuple-element.10), channel_id=1, source_target_pairs={{0,0},{1,1},{2,32},{3,33},{4,64},{5,65},{6,96},{7,97},{8,128},{9,1... | collective-permute-start | bytes 73736 | tf_op jit(solution)/shard_map/ppermute | solution.py:211
  3.9 30.3 %collective-permute-start = (bf16[192,128]{1,0:T(8,128)(2,1)}, bf16[192,128]{1,0:T(8,128)(2,1)S(1)}, u32[]{:S(2)}, u32[]{:S(2)}) collective-permute-start(bf16[192,128]{1,0:T(8,128)(2,1)} %get-tuple-element.9.own_ref.nq_ref), channel_id=1, source_target_pairs={{0,8},{1,9},{2,10},{3,11},{4,12},{5,13},{6,14},{7,15},{8,0},{9,1},... | collective-permute-start | bytes 147464 | tf_op jit(solution)/shard_map/ppermute | solution.py:202
  13.2 21.0 %collective-permute-start.1 = (bf16[192,128]{1,0:T(8,128)(2,1)}, bf16[192,128]{1,0:T(8,128)(2,1)S(1)}, u32[]{:S(2)}, u32[]{:S(2)}) collective-permute-start(bf16[192,128]{1,0:T(8,128)(2,1)} %get-tuple-element.9.own_ref.nq_ref), channel_id=1, source_target_pairs={{0,24},{1,25},{2,26},{3,27},{4,28},{5,29},{6,30},{7,31},{8,16},{9,... | collective-permute-start | bytes 147464 | tf_op jit(solution)/shard_map/ppermute | solution.py:202
  23.2 11.0 %collective-permute-start.2 = (bf16[192,128]{1,0:T(8,128)(2,1)}, bf16[192,128]{1,0:T(8,128)(2,1)S(1)}, u32[]{:S(2)}, u32[]{:S(2)}) collective-permute-start(bf16[192,128]{1,0:T(8,128)(2,1)} %get-tuple-element.9.own_ref.nq_ref), channel_id=1, source_target_pairs={{0,16},{1,17},{2,18},{3,19},{4,20},{5,21},{6,22},{7,23},{8,24},{9,... | collective-permute-start | bytes 147464 | tf_op jit(solution)/shard_map/ppermute | solution.py:202
  26.1 8.1 %copy-start.1 = (bf16[192,128]{1,0:T(8,128)(2,1)S(1)}, bf16[192,128]{1,0:T(8,128)(2,1)}, u32[]{:S(2)}) copy-start(bf16[192,128]{1,0:T(8,128)(2,1)} %get-tuple-element.9.own_ref.nq_ref) | copy-start | bytes 147460
  26.1 25.5 %all-to-all-start = ((f32[16,48,128]{2,1,0:T(8,128)}), f32[16,48,128]{2,1,0:T(8,128)S(1)}, u32[]{:S(2)}, u32[]{:S(2)}) async-start(f32[16,48,128]{2,1,0:T(8,128)} %copies.1), calls=%async_computation | async-start | bytes 786432 | tf_op jit(solution)/shard_map/all_to_all | solution.py:252
  34.2 6.7 %collective-permute-start.3 = (bf16[768,128]{1,0:T(8,128)(2,1)S(1)}, bf16[768,128]{1,0:T(8,128)(2,1)S(1)}, u32[]{:S(2)}, u32[]{:S(2)}) collective-permute-start(bf16[768,128]{1,0:T(8,128)(2,1)S(1)} %relay.1.own_ref), channel_id=1, source_target_pairs={{0,2},{1,3},{2,0},{3,1},{4,6},{5,7},{6,4},{7,5},{8,10},{9,11},{10,... | collective-permute-start | bytes 589832 | tf_op jit(solution)/shard_map/ppermute | solution.py:202
  37.5 7.9 %collective-permute-start.4 = (bf16[768,128]{1,0:T(8,128)(2,1)S(1)}, bf16[768,128]{1,0:T(8,128)(2,1)S(1)}, u32[]{:S(2)}, u32[]{:S(2)}) collective-permute-start(bf16[768,128]{1,0:T(8,128)(2,1)S(1)} %relay.1.own_ref), channel_id=1, source_target_pairs={{0,6},{1,7},{2,4},{3,5},{4,2},{5,3},{6,0},{7,1},{8,14},{9,15},{10,... | collective-permute-start | bytes 589832 | tf_op jit(solution)/shard_map/ppermute | solution.py:202
  41.0 10.6 %collective-permute-start.5 = (bf16[768,128]{1,0:T(8,128)(2,1)S(1)}, bf16[768,128]{1,0:T(8,128)(2,1)S(1)}, u32[]{:S(2)}, u32[]{:S(2)}) collective-permute-start(bf16[768,128]{1,0:T(8,128)(2,1)S(1)} %collective-permute-done.3.first_ref), channel_id=1, source_target_pairs={{0,6},{1,7},{2,4},{3,5},{4,2},{5,3},{6,0},{7,1},{8,14},{9,15},{10,... | collective-permute-start | bytes 589832 | tf_op jit(solution)/shard_map/ppermute | solution.py:202
  45.5 9.1 %collective-permute-start.6 = (bf16[3,768,128]{2,1,0:T(8,128)(2,1)S(1)}, bf16[3,768,128]{2,1,0:T(8,128)(2,1)S(1)}, u32[]{:S(2)}, u32[]{:S(2)}) collective-permute-start(bf16[3,768,128]{2,1,0:T(8,128)(2,1)S(1)} %pad_maximum_fusion), channel_id=1, source_target_pairs={{0,1},{1,0},{2,3},{3,2},{4,5},{5,4},{6,7},{7,6},{8,9},{9,8},{10,11... | collective-permute-start | bytes 1769480 | tf_op jit(solution)/shard_map/ppermute | solution.py:202
  51.5 4.5 %copy-start = (bf16[128,256]{1,0:T(8,128)(2,1)S(1)}, bf16[128,256]{1,0:T(8,128)(2,1)}, u32[]{:S(2)}) copy-start(bf16[128,256]{1,0:T(8,128)(2,1)} %wkv_ref.1) | copy-start | bytes 196612
  51.6 4.5 %copy-start.2 = (bf16[128,128]{1,0:T(8,128)(2,1)S(1)}, bf16[128,128]{1,0:T(8,128)(2,1)}, u32[]{:S(2)}) copy-start(bf16[128,128]{1,0:T(8,128)(2,1)} %wq_ref.1) | copy-start | bytes 98308
  51.6 4.5 %copy-start.3 = (bf16[128,128]{1,0:T(8,128)(2,1)S(1)}, bf16[128,128]{1,0:T(8,128)(2,1)}, u32[]{:S(2)}) copy-start(bf16[128,128]{1,0:T(8,128)(2,1)} %wg_ref.1) | copy-start | bytes 98308
  51.6 4.5 %copy-start.4 = (bf16[128,128]{1,0:T(8,128)(2,1)S(1)}, bf16[128,128]{1,0:T(8,128)(2,1)}, u32[]{:S(2)}) copy-start(bf16[128,128]{1,0:T(8,128)(2,1)} %wo_ref.1) | copy-start | bytes 98308
  51.7 4.4 %collective-permute-start.8 = (bf16[1920,128]{1,0:T(8,128)(2,1)S(1)}, bf16[1920,128]{1,0:T(8,128)(2,1)S(1)}, u32[]{:S(2)}, u32[]{:S(2)}) collective-permute-start(bf16[1920,128]{1,0:T(8,128)(2,1)S(1)} %get-tuple-element.11), channel_id=1, source_target_pairs={{0,1},{1,0},{2,3},{3,2},{4,5},{5,4},{6,7},{7,6},{8,9},{9,8},{10,11... | collective-permute-start | bytes 1474568 | tf_op jit(solution)/shard_map/ppermute | solution.py:202
where the time goes:
time: 61.2 us; the launch traced here: 60.4 us
  starting transfers between devices  50 us (82%)
  Pallas kernels  7.81 us (13%)
  waiting for transfers between devices  2.21 us (4%)
    ppermute x8, starting transfers between devices, permute_col(): return lax.ppermute(value, 'col', [(c, target(c)) for c in range(NCOL)])  40.5 us
    all_to_all x1, starting transfers between devices, body(): bias = lax.all_to_all(tiles, 'row', 0, 0)  8.09 us
    pallas_call x1, Pallas kernels, body(): pl.pallas_call(attend_kernel, in_specs=[whole()] * 12, out_specs=whole(),...  4.28 us
    pallas_call x1, Pallas kernels, body(): pl.pallas_call(front_kernel, in_specs=[whole(pl.ANY)] * 3, out_specs=[who...  2.5 us
    ppermute x8, waiting for transfers between devices, permute_col(): return lax.ppermute(value, 'col', [(c, target(c)) for c in range(NCOL)])  2.21 us
    ppermute x1, starting transfers between devices, permute_all(): return lax.ppermute(value, ('row', 'col'), pairs)  1.4 us
  transfers between devices with their start and end apart: 10, of which 3 were waited for; matrix products, arithmetic and copies ran while one was open for 0% of the time, Pallas kernels for 2%

commit v1 on v0

--- a/solution.py
+++ b/solution.py
@@ -91,6 +91,7 @@
 
 
 HALF_K = NROW * KB
+GROUP = HEADS * KB
 
 
 def join_kernel(third_ref, bias_ref, payload_ref, order_ref):
@@ -137,20 +138,25 @@
         own_ref, first_ref, second_ref, third_ref,
         theirs_a_ref.at[0], theirs_a_ref.at[1], theirs_a_ref.at[2], theirs_b_ref,
     )
-    bias_ref[0:HALF_K, :] = order_ref[...]
     terms = []
     for term in range(3):
         begin = third_ref.shape[0] + term * HALF_K
         terms.append(theirs_b_ref[begin : begin + HALF_K, :].astype(F32))
-    bias_ref[HALF_K:, :] = (terms[0] + terms[1]) + terms[2]
+    theirs = (terms[0] + terms[1]) + terms[2]
+    for part in range(HALF_K // LANES):
+        span = slice(part * LANES, (part + 1) * LANES)
+        bias_ref[:, span] = order_ref[span, :].T[:GROUP, :]
+        bias_ref[:, HALF_K + part * LANES : HALF_K + (part + 1) * LANES] = theirs[span, :].T[
+            :GROUP, :
+        ]
     nq = nq_ref[...]
     query = jnp.dot(nq, wq_ref[...], preferred_element_type=F32) * (1.0 / 32**0.5)
     query = query.astype(BF16).astype(F32)
     gate_ref[...] = jax.nn.sigmoid(jnp.dot(nq, wg_ref[...], preferred_element_type=F32))
     wk = twice(wkv_ref[:, :LANES].astype(F32)).astype(BF16)
-    wvt = twice(wkv_ref[:, LANES:].astype(F32).T).astype(BF16)
+    wv = twice(wkv_ref[:, LANES:].astype(F32)).astype(BF16)
     lane = lax.broadcasted_iota(jnp.int32, (KB, LANES), 1)
-    zero = jnp.zeros((LANES, LANES), F32)
+    zero = jnp.zeros((GROUP, LANES), F32)
     for i in range(QROWS // 2):
         sides = []
         masked = []
@@ -160,7 +166,6 @@
             )
             q = query[a * KB : (a + 1) * KB, :]
             parts = [jnp.where(lane // 32 == h, q, 0.0) for h in range(HEADS)]
-            parts.append(jnp.zeros((LANES - HEADS * KB, LANES), F32))
             masked.append(jnp.concatenate(parts, axis=0))
         queries = jnp.concatenate(
             [
@@ -171,23 +176,23 @@
         ).astype(BF16)
         rows = jnp.concatenate(sides, axis=1)
         keys = jnp.dot(rows, wk, preferred_element_type=F32).astype(BF16)
-        values_t = nt_dot(wvt, rows).astype(BF16)
-        score = nt_dot(keys, queries)
+        values = jnp.dot(rows, wv, preferred_element_type=F32).astype(BF16)
+        score = nt_dot(queries, keys)
         for n in range(2):
             a = 2 * i + n
-            full = score[:, n * LANES : (n + 1) * LANES] + bias_ref[...]
+            full = score[n * GROUP : (n + 1) * GROUP, :] + bias_ref[...]
             held_ref[a % 4] = full
-            top = jnp.max(full, axis=0, keepdims=True)
+            top = jnp.max(full, axis=1, keepdims=True)
             weights = jnp.exp(held_ref[a % 4] - top)
-            total = jnp.sum(weights, axis=0, keepdims=True)
+            total = jnp.sum(weights, axis=1, keepdims=True)
             high = weights.astype(BF16)
             low = (weights - high.astype(F32)).astype(BF16)
             both = jnp.dot(
-                values_t[n * LANES : (n + 1) * LANES, :],
-                jnp.concatenate([high, low], axis=1),
+                jnp.concatenate([high, low], axis=0),
+                values[:, n * LANES : (n + 1) * LANES],
                 preferred_element_type=F32,
             )
-            attended = ((both[:, :LANES] + both[:, LANES:]) / total).T
+            attended = (both[:GROUP, :] + both[GROUP:, :]) / total
             mine = jnp.zeros((KB, LANES), F32)
             for h in range(HEADS):
                 mine = jnp.where(lane // 32 == h, attended[h * KB : (h + 1) * KB, :], mine)
@@ -281,8 +286,8 @@
         out_specs=whole(),
         out_shape=shape((nrows, LANES), BF16),
         scratch_shapes=[
-            VM((N_RES, LANES), F32),
-            VM((4, 768, LANES), F32),
+            VM((GROUP, N_RES), F32),
+            VM((4, GROUP, N_RES), F32),
             VM((nrows, LANES), F32),
             VM((nrows, LANES), F32),
         ],

time: 61.2 us -> 60.7 us (level)
  no operation moved by 1% of the time
where the time goes in v1:
time: 60.7 us; the launch traced here: 59.9 us
  starting transfers between devices  50 us (82%)
  Pallas kernels  7.32 us (12%)
  waiting for transfers between devices  2.21 us (4%)
    ppermute x8, starting transfers between devices, permute_col(): return lax.ppermute(value, 'col', [(c, target(c)) for c in range(NCOL)])  40.5 us
    all_to_all x1, starting transfers between devices, body(): bias = lax.all_to_all(tiles, 'row', 0, 0)  8.09 us
    pallas_call x1, Pallas kernels, body(): pl.pallas_call(attend_kernel, in_specs=[whole()] * 12, out_specs=whole(),...  3.79 us
    pallas_call x1, Pallas kernels, body(): pl.pallas_call(front_kernel, in_specs=[whole(pl.ANY)] * 3, out_specs=[who...  2.5 us
    ppermute x8, waiting for transfers between devices, permute_col(): return lax.ppermute(value, 'col', [(c, target(c)) for c in range(NCOL)])  2.21 us
    ppermute x1, starting transfers between devices, permute_all(): return lax.ppermute(value, ('row', 'col'), pairs)  1.4 us
  transfers between devices with their start and end apart: 10, of which 3 were waited for; matrix products, arithmetic and copies ran while one was open for 0% of the time, Pallas kernels for 2%

profile of v1, /device:TPU:1, one launch (start us, length us, event | category | flops | bytes accessed | tf_op | source)
XLA Modules:
  0.0 59.9 jit_solution(2675463270500687109)
XLA Ops:
  0.0 2.5 %front.1 = (bf16[192,128]{1,0:T(8,128)(2,1)}, f32[48,128]{1,0:T(8,128)}) custom-call(bf16[1152,128]{1,0:T(8,128)(2,1)} %bitcast.12, f32[1,128]{1,0:T(1,128)} %bitcast.14, bf16[4,128]{1,0:T(4,128)(2,1)} %bitcast.13), custom_call_target="tpu_custom_call" | custom-call | tf_op jit(solution)/shard_map/front/pallas_call | solution.py:231
  2.5 1.4 %collective-permute-start.7 = (f32[48,128]{1,0:T(8,128)}, f32[48,128]{1,0:T(8,128)S(1)}, u32[]{:S(2)}, u32[]{:S(2)}) collective-permute-start(f32[48,128]{1,0:T(8,128)} %get-tuple-element.10), channel_id=1, source_target_pairs={{0,0},{1,1},{2,32},{3,33},{4,64},{5,65},{6,96},{7,97},{8,128},{9,1... | collective-permute-start | bytes 73736 | tf_op jit(solution)/shard_map/ppermute | solution.py:216
  3.9 9.2 %collective-permute-start = (bf16[192,128]{1,0:T(8,128)(2,1)}, bf16[192,128]{1,0:T(8,128)(2,1)S(1)}, u32[]{:S(2)}, u32[]{:S(2)}) collective-permute-start(bf16[192,128]{1,0:T(8,128)(2,1)} %get-tuple-element.9.own_ref.nq_ref), channel_id=1, source_target_pairs={{0,8},{1,9},{2,10},{3,11},{4,12},{5,13},{6,14},{7,15},{8,0},{9,1},... | collective-permute-start | bytes 147464 | tf_op jit(solution)/shard_map/ppermute | solution.py:207
  13.2 10.0 %collective-permute-start.1 = (bf16[192,128]{1,0:T(8,128)(2,1)}, bf16[192,128]{1,0:T(8,128)(2,1)S(1)}, u32[]{:S(2)}, u32[]{:S(2)}) collective-permute-start(bf16[192,128]{1,0:T(8,128)(2,1)} %get-tuple-element.9.own_ref.nq_ref), channel_id=1, source_target_pairs={{0,24},{1,25},{2,26},{3,27},{4,28},{5,29},{6,30},{7,31},{8,16},{9,... | collective-permute-start | bytes 147464 | tf_op jit(solution)/shard_map/ppermute | solution.py:207
  23.2 1.9 %collective-permute-start.2 = (bf16[192,128]{1,0:T(8,128)(2,1)}, bf16[192,128]{1,0:T(8,128)(2,1)S(1)}, u32[]{:S(2)}, u32[]{:S(2)}) collective-permute-start(bf16[192,128]{1,0:T(8,128)(2,1)} %get-tuple-element.9.own_ref.nq_ref), channel_id=1, source_target_pairs={{0,16},{1,17},{2,18},{3,19},{4,20},{5,21},{6,22},{7,23},{8,24},{9,... | collective-permute-start | bytes 147464 | tf_op jit(solution)/shard_map/ppermute | solution.py:207
  25.1 0.9 %copies.1 = f32[16,48,128]{2,1,0:T(8,128)} custom-call(f32[48,128]{1,0:T(8,128)S(1)} %collective-permute-done.7.tile_ref), custom_call_target="tpu_custom_call" | custom-call | flops 20000000000 | tf_op jit(solution)/shard_map/copies/pallas_call | solution.py:247
  26.1 0.0 copy-start.1
  26.1 8.1 %all-to-all-start = ((f32[16,48,128]{2,1,0:T(8,128)}), f32[16,48,128]{2,1,0:T(8,128)S(1)}, u32[]{:S(2)}, u32[]{:S(2)}) async-start(f32[16,48,128]{2,1,0:T(8,128)} %copies.1), calls=%async_computation | async-start | bytes 786432 | tf_op jit(solution)/shard_map/all_to_all | solution.py:257
  34.2 0.0 collective-permute-done.first_ref
  34.2 3.2 %collective-permute-start.3 = (bf16[768,128]{1,0:T(8,128)(2,1)S(1)}, bf16[768,128]{1,0:T(8,128)(2,1)S(1)}, u32[]{:S(2)}, u32[]{:S(2)}) collective-permute-start(bf16[768,128]{1,0:T(8,128)(2,1)S(1)} %relay.1.own_ref), channel_id=1, source_target_pairs={{0,2},{1,3},{2,0},{3,1},{4,6},{5,7},{6,4},{7,5},{8,10},{9,11},{10,... | collective-permute-start | bytes 589832 | tf_op jit(solution)/shard_map/ppermute | solution.py:207
  37.5 3.2 %collective-permute-start.4 = (bf16[768,128]{1,0:T(8,128)(2,1)S(1)}, bf16[768,128]{1,0:T(8,128)(2,1)S(1)}, u32[]{:S(2)}, u32[]{:S(2)}) collective-permute-start(bf16[768,128]{1,0:T(8,128)(2,1)S(1)} %relay.1.own_ref), channel_id=1, source_target_pairs={{0,6},{1,7},{2,4},{3,5},{4,2},{5,3},{6,0},{7,1},{8,14},{9,15},{10,... | collective-permute-start | bytes 589832 | tf_op jit(solution)/shard_map/ppermute | solution.py:207
  40.7 0.3 collective-permute-done.3.first_ref
  41.0 4.0 %collective-permute-start.5 = (bf16[768,128]{1,0:T(8,128)(2,1)S(1)}, bf16[768,128]{1,0:T(8,128)(2,1)S(1)}, u32[]{:S(2)}, u32[]{:S(2)}) collective-permute-start(bf16[768,128]{1,0:T(8,128)(2,1)S(1)} %collective-permute-done.3.first_ref), channel_id=1, source_target_pairs={{0,6},{1,7},{2,4},{3,5},{4,2},{5,3},{6,0},{7,1},{8,14},{9,15},{10,... | collective-permute-start | bytes 589832 | tf_op jit(solution)/shard_map/ppermute | solution.py:207
  45.0 0.4 collective-permute-done.4.second_ref
  45.4 0.1 pad_maximum_fusion
  45.5 6.0 %collective-permute-start.6 = (bf16[3,768,128]{2,1,0:T(8,128)(2,1)S(1)}, bf16[3,768,128]{2,1,0:T(8,128)(2,1)S(1)}, u32[]{:S(2)}, u32[]{:S(2)}) collective-permute-start(bf16[3,768,128]{2,1,0:T(8,128)(2,1)S(1)} %pad_maximum_fusion), channel_id=1, source_target_pairs={{0,1},{1,0},{2,3},{3,2},{4,5},{5,4},{6,7},{7,6},{8,9},{9,8},{10,11... | collective-permute-start | bytes 1769480 | tf_op jit(solution)/shard_map/ppermute | solution.py:207
  51.5 0.0 copy-start
  51.6 0.0 copy-start.2
  51.6 0.0 copy-start.3
  51.6 0.0 copy-start.4
  51.6 0.1 join.1
  51.7 2.9 %collective-permute-start.8 = (bf16[1920,128]{1,0:T(8,128)(2,1)S(1)}, bf16[1920,128]{1,0:T(8,128)(2,1)S(1)}, u32[]{:S(2)}, u32[]{:S(2)}) collective-permute-start(bf16[1920,128]{1,0:T(8,128)(2,1)S(1)} %get-tuple-element.11), channel_id=1, source_target_pairs={{0,1},{1,0},{2,3},{3,2},{4,5},{5,4},{6,7},{7,6},{8,9},{9,8},{10,11... | collective-permute-start | bytes 1474568 | tf_op jit(solution)/shard_map/ppermute | solution.py:207
  54.6 1.5 %collective-permute-done.8.theirs_b_ref = bf16[1920,128]{1,0:T(8,128)(2,1)S(1)} collective-permute-done((bf16[1920,128]{1,0:T(8,128)(2,1)S(1)}, bf16[1920,128]{1,0:T(8,128)(2,1)S(1)}, u32[]{:S(2)}, u32[]{:S(2)}) %collective-permute-start.8) | collective-permute-done | bytes 491552 | tf_op jit(solution)/shard_map/ppermute | solution.py:207
  56.1 3.8 %attend.1 = bf16[192,128]{1,0:T(8,128)(2,1)} custom-call(bf16[768,128]{1,0:T(8,128)(2,1)S(1)} %relay.1.own_ref, bf16[768,128]{1,0:T(8,128)(2,1)S(1)} %collective-permute-done.3.first_ref, bf16[768,128]{1,0:T(8,128)(2,1)S(1)} %collective-permute-done.4.second_ref, bf16[768,128]{1,0:T(8,128)(2,1)S(1)} %collective-permute-done.5.third_ref, ...), custom_call_target="tpu_custom_call" | custom-call | tf_op jit(solution)/shard_map/attend/pallas_call | solution.py:283
  (12 shorter events, 0.1 us)
Async XLA Ops:
  2.5 22.6 %collective-permute-start.7 = (f32[48,128]{1,0:T(8,128)}, f32[48,128]{1,0:T(8,128)S(1)}, u32[]{:S(2)}, u32[]{:S(2)}) collective-permute-start(f32[48,128]{1,0:T(8,128)} %get-tuple-element.10), channel_id=1, source_target_pairs={{0,0},{1,1},{2,32},{3,33},{4,64},{5,65},{6,96},{7,97},{8,128},{9,1... | collective-permute-start | bytes 73736 | tf_op jit(solution)/shard_map/ppermute | solution.py:216
  3.9 30.3 %collective-permute-start = (bf16[192,128]{1,0:T(8,128)(2,1)}, bf16[192,128]{1,0:T(8,128)(2,1)S(1)}, u32[]{:S(2)}, u32[]{:S(2)}) collective-permute-start(bf16[192,128]{1,0:T(8,128)(2,1)} %get-tuple-element.9.own_ref.nq_ref), channel_id=1, source_target_pairs={{0,8},{1,9},{2,10},{3,11},{4,12},{5,13},{6,14},{7,15},{8,0},{9,1},... | collective-permute-start | bytes 147464 | tf_op jit(solution)/shard_map/ppermute | solution.py:207
  13.2 21.0 %collective-permute-start.1 = (bf16[192,128]{1,0:T(8,128)(2,1)}, bf16[192,128]{1,0:T(8,128)(2,1)S(1)}, u32[]{:S(2)}, u32[]{:S(2)}) collective-permute-start(bf16[192,128]{1,0:T(8,128)(2,1)} %get-tuple-element.9.own_ref.nq_ref), channel_id=1, source_target_pairs={{0,24},{1,25},{2,26},{3,27},{4,28},{5,29},{6,30},{7,31},{8,16},{9,... | collective-permute-start | bytes 147464 | tf_op jit(solution)/shard_map/ppermute | solution.py:207
  23.2 11.0 %collective-permute-start.2 = (bf16[192,128]{1,0:T(8,128)(2,1)}, bf16[192,128]{1,0:T(8,128)(2,1)S(1)}, u32[]{:S(2)}, u32[]{:S(2)}) collective-permute-start(bf16[192,128]{1,0:T(8,128)(2,1)} %get-tuple-element.9.own_ref.nq_ref), channel_id=1, source_target_pairs={{0,16},{1,17},{2,18},{3,19},{4,20},{5,21},{6,22},{7,23},{8,24},{9,... | collective-permute-start | bytes 147464 | tf_op jit(solution)/shard_map/ppermute | solution.py:207
  26.1 8.1 %copy-start.1 = (bf16[192,128]{1,0:T(8,128)(2,1)S(1)}, bf16[192,128]{1,0:T(8,128)(2,1)}, u32[]{:S(2)}) copy-start(bf16[192,128]{1,0:T(8,128)(2,1)} %get-tuple-element.9.own_ref.nq_ref) | copy-start | bytes 147460
  26.1 25.5 %all-to-all-start = ((f32[16,48,128]{2,1,0:T(8,128)}), f32[16,48,128]{2,1,0:T(8,128)S(1)}, u32[]{:S(2)}, u32[]{:S(2)}) async-start(f32[16,48,128]{2,1,0:T(8,128)} %copies.1), calls=%async_computation | async-start | bytes 786432 | tf_op jit(solution)/shard_map/all_to_all | solution.py:257
  34.2 6.7 %collective-permute-start.3 = (bf16[768,128]{1,0:T(8,128)(2,1)S(1)}, bf16[768,128]{1,0:T(8,128)(2,1)S(1)}, u32[]{:S(2)}, u32[]{:S(2)}) collective-permute-start(bf16[768,128]{1,0:T(8,128)(2,1)S(1)} %relay.1.own_ref), channel_id=1, source_target_pairs={{0,2},{1,3},{2,0},{3,1},{4,6},{5,7},{6,4},{7,5},{8,10},{9,11},{10,... | collective-permute-start | bytes 589832 | tf_op jit(solution)/shard_map/ppermute | solution.py:207
  37.5 7.9 %collective-permute-start.4 = (bf16[768,128]{1,0:T(8,128)(2,1)S(1)}, bf16[768,128]{1,0:T(8,128)(2,1)S(1)}, u32[]{:S(2)}, u32[]{:S(2)}) collective-permute-start(bf16[768,128]{1,0:T(8,128)(2,1)S(1)} %relay.1.own_ref), channel_id=1, source_target_pairs={{0,6},{1,7},{2,4},{3,5},{4,2},{5,3},{6,0},{7,1},{8,14},{9,15},{10,... | collective-permute-start | bytes 589832 | tf_op jit(solution)/shard_map/ppermute | solution.py:207
  41.0 10.6 %collective-permute-start.5 = (bf16[768,128]{1,0:T(8,128)(2,1)S(1)}, bf16[768,128]{1,0:T(8,128)(2,1)S(1)}, u32[]{:S(2)}, u32[]{:S(2)}) collective-permute-start(bf16[768,128]{1,0:T(8,128)(2,1)S(1)} %collective-permute-done.3.first_ref), channel_id=1, source_target_pairs={{0,6},{1,7},{2,4},{3,5},{4,2},{5,3},{6,0},{7,1},{8,14},{9,15},{10,... | collective-permute-start | bytes 589832 | tf_op jit(solution)/shard_map/ppermute | solution.py:207
  45.5 9.1 %collective-permute-start.6 = (bf16[3,768,128]{2,1,0:T(8,128)(2,1)S(1)}, bf16[3,768,128]{2,1,0:T(8,128)(2,1)S(1)}, u32[]{:S(2)}, u32[]{:S(2)}) collective-permute-start(bf16[3,768,128]{2,1,0:T(8,128)(2,1)S(1)} %pad_maximum_fusion), channel_id=1, source_target_pairs={{0,1},{1,0},{2,3},{3,2},{4,5},{5,4},{6,7},{7,6},{8,9},{9,8},{10,11... | collective-permute-start | bytes 1769480 | tf_op jit(solution)/shard_map/ppermute | solution.py:207
  51.5 4.5 %copy-start = (bf16[128,256]{1,0:T(8,128)(2,1)S(1)}, bf16[128,256]{1,0:T(8,128)(2,1)}, u32[]{:S(2)}) copy-start(bf16[128,256]{1,0:T(8,128)(2,1)} %wkv_ref.1) | copy-start | bytes 196612
  51.6 4.5 %copy-start.2 = (bf16[128,128]{1,0:T(8,128)(2,1)S(1)}, bf16[128,128]{1,0:T(8,128)(2,1)}, u32[]{:S(2)}) copy-start(bf16[128,128]{1,0:T(8,128)(2,1)} %wq_ref.1) | copy-start | bytes 98308
  51.6 4.5 %copy-start.3 = (bf16[128,128]{1,0:T(8,128)(2,1)S(1)}, bf16[128,128]{1,0:T(8,128)(2,1)}, u32[]{:S(2)}) copy-start(bf16[128,128]{1,0:T(8,128)(2,1)} %wg_ref.1) | copy-start | bytes 98308
  51.6 4.5 %copy-start.4 = (bf16[128,128]{1,0:T(8,128)(2,1)S(1)}, bf16[128,128]{1,0:T(8,128)(2,1)}, u32[]{:S(2)}) copy-start(bf16[128,128]{1,0:T(8,128)(2,1)} %wo_ref.1) | copy-start | bytes 98308
  51.7 4.4 %collective-permute-start.8 = (bf16[1920,128]{1,0:T(8,128)(2,1)S(1)}, bf16[1920,128]{1,0:T(8,128)(2,1)S(1)}, u32[]{:S(2)}, u32[]{:S(2)}) collective-permute-start(bf16[1920,128]{1,0:T(8,128)(2,1)S(1)} %get-tuple-element.11), channel_id=1, source_target_pairs={{0,1},{1,0},{2,3},{3,2},{4,5},{5,4},{6,7},{7,6},{8,9},{9,8},{10,11... | collective-permute-start | bytes 1474568 | tf_op jit(solution)/shard_map/ppermute | solution.py:207

commit v2 on v1

--- a/solution.py
+++ b/solution.py
@@ -82,10 +82,10 @@
         send.wait()
 
 
-def relay_kernel(own_ref, first_ref, second_ref, third_ref, out_ref):
+def relay_kernel(own_ref, near_ref, far_ref, out_ref):
     for a in range(QROWS):
         span = slice(a * KB, (a + 1) * KB)
-        refs = (own_ref, first_ref, second_ref, third_ref)
+        refs = (own_ref, near_ref, far_ref.at[0], far_ref.at[1])
         parts = [ref[span, :].astype(F32) for ref in refs]
         out_ref[a * 96 : (a + 1) * 96, :] = jnp.concatenate(parts, axis=0).astype(BF16)
 
@@ -241,7 +241,8 @@
         ],
         name="front",
     )(rows, ln_gain.reshape(1, LANES), w_bias.T)
-    ys = [nq] + [permute_col(nq, near_y(mask)) for mask in MASKS[1:]]
+    near = permute_col(nq, near_y(1))
+    far = permute_col(jnp.stack([nq, near]), near_y(3))
     tile = permute_all(tile, lambda r, c: (c // 2, 2 * r + c % 2))
     small = pltpu.CompilerParams(vmem_limit_bytes=16 * 1024 * 1024)
     tiles = pl.pallas_call(
@@ -257,13 +258,13 @@
     bias = lax.all_to_all(tiles, "row", 0, 0)
     piece = pl.pallas_call(
         relay_kernel,
-        in_specs=[whole()] * 4,
+        in_specs=[whole()] * 3,
         out_specs=whole(),
         out_shape=shape((4 * nrows, LANES), BF16),
         compiler_params=small,
         cost_estimate=pl.CostEstimate(flops=30 * 10**9, bytes_accessed=0, transcendentals=0),
         name="relay",
-    )(*ys)
+    )(nq, near, far)
     first = permute_col(piece, near_x(1))
     second = permute_col(piece, near_x(3))
     third = permute_col(first, near_x(3))

time: 60.7 us -> 62.3 us (1.026)
  waiting for transfers between devices: 2.21 us -> 3.8 us
  other arithmetic: 0.07 us -> 0.88 us
    ppermute x8 -> x7, waiting for transfers between devices: 2.21 us -> 3.8 us  [permute_col(): return lax.ppermute(value, 'col', [(c, target(c)) for c in range(NCOL)])]
    ppermute x8 -> x7, starting transfers between devices: 40.5 us -> 39.3 us  [permute_col(): return lax.ppermute(value, 'col', [(c, target(c)) for c in range(NCOL)])]
    another operation x0 -> x1, other arithmetic: none -> 0.81 us  [body(): far = permute_col(jnp.stack([nq, near]), near_y(3))]
    all_to_all x1, starting transfers between devices: 8.09 us -> 8.77 us  [body(): bias = lax.all_to_all(tiles, 'row', 0, 0)]
  transfers between devices with their start and end apart: 10 -> 9, of which waited for: 3 -> 4; matrix products, arithmetic and copies ran while one was open for 0% -> 1% of each run, Pallas kernels for 2% -> 2%
where the time goes in v2:
time: 62.3 us; the launch traced here: 61.7 us
  starting transfers between devices  49.5 us (79%)
  Pallas kernels  7.33 us (12%)
  waiting for transfers between devices  3.8 us (6%)
  other arithmetic  0.88 us (1%)
    ppermute x7, starting transfers between devices, permute_col(): return lax.ppermute(value, 'col', [(c, target(c)) for c in range(NCOL)])  39.3 us
    all_to_all x1, starting transfers between devices, body(): bias = lax.all_to_all(tiles, 'row', 0, 0)  8.77 us
    ppermute x7, waiting for transfers between devices, permute_col(): return lax.ppermute(value, 'col', [(c, target(c)) for c in range(NCOL)])  3.8 us
    pallas_call x1, Pallas kernels, body(): pl.pallas_call(attend_kernel, in_specs=[whole()] * 12, out_specs=whole(),...  3.8 us
    pallas_call x1, Pallas kernels, body(): pl.pallas_call(front_kernel, in_specs=[whole(pl.ANY)] * 3, out_specs=[who...  2.5 us
    ppermute x1, starting transfers between devices, permute_all(): return lax.ppermute(value, ('row', 'col'), pairs)  1.4 us
  transfers between devices with their start and end apart: 9, of which 4 were waited for; matrix products, arithmetic and copies ran while one was open for 1% of the time, Pallas kernels for 2%

profile of v2, /device:TPU:1, one launch (start us, length us, event | category | flops | bytes accessed | tf_op | source)
XLA Modules:
  0.0 61.7 jit_solution(9342705630271776750)
XLA Ops:
  0.0 2.5 %front.1 = (bf16[192,128]{1,0:T(8,128)(2,1)}, f32[48,128]{1,0:T(8,128)}) custom-call(bf16[1152,128]{1,0:T(8,128)(2,1)} %bitcast.16, f32[1,128]{1,0:T(1,128)} %bitcast.18, bf16[4,128]{1,0:T(4,128)(2,1)} %bitcast.17), custom_call_target="tpu_custom_call" | custom-call | tf_op jit(solution)/shard_map/front/pallas_call | solution.py:231
  2.5 5.0 %collective-permute-start = (bf16[192,128]{1,0:T(8,128)(2,1)}, bf16[192,128]{1,0:T(8,128)(2,1)S(1)}, u32[]{:S(2)}, u32[]{:S(2)}) collective-permute-start(bf16[192,128]{1,0:T(8,128)(2,1)} %get-tuple-element.9.own_ref.nq_ref), channel_id=1, source_target_pairs={{0,8},{1,9},{2,10},{3,11},{4,12},{5,13},{6,14},{7,15},{8,0},{9,1},... | collective-permute-start | bytes 147464 | tf_op jit(solution)/shard_map/ppermute | solution.py:207
  7.6 1.4 %collective-permute-start.6 = (f32[48,128]{1,0:T(8,128)}, f32[48,128]{1,0:T(8,128)S(1)}, u32[]{:S(2)}, u32[]{:S(2)}) collective-permute-start(f32[48,128]{1,0:T(8,128)} %get-tuple-element.10), channel_id=1, source_target_pairs={{0,0},{1,1},{2,32},{3,33},{4,64},{5,65},{6,96},{7,97},{8,128},{9,1... | collective-permute-start | bytes 73736 | tf_op jit(solution)/shard_map/ppermute | solution.py:216
  9.0 0.3 collective-permute-done.near_ref
  9.2 0.8 %pad_maximum_fusion.1 = bf16[2,192,128]{2,1,0:T(8,128)(2,1)S(1)} fusion(bf16[1,192,128]{2,1,0:T(8,128)(2,1)S(1)} %bitcast.15, bf16[1,192,128]{2,1,0:T(8,128)(2,1)} %bitcast.14), kind=kLoop, calls=%fused_computation.1 | loop fusion | flops 49152 | bytes 196608 | tf_op jit(solution)/shard_map/stack | solution.py:245
  10.1 14.2 %collective-permute-start.1 = (bf16[2,192,128]{2,1,0:T(8,128)(2,1)S(1)}, bf16[2,192,128]{2,1,0:T(8,128)(2,1)S(1)}, u32[]{:S(2)}, u32[]{:S(2)}) collective-permute-start(bf16[2,192,128]{2,1,0:T(8,128)(2,1)S(1)} %pad_maximum_fusion.1), channel_id=1, source_target_pairs={{0,24},{1,25},{2,26},{3,27},{4,28},{5,29},{6,30},{7,31},{8,16},{9,... | collective-permute-start | bytes 294920 | tf_op jit(solution)/shard_map/ppermute | solution.py:207
  24.3 0.9 %copies.1 = f32[16,48,128]{2,1,0:T(8,128)} custom-call(f32[48,128]{1,0:T(8,128)S(1)} %collective-permute-done.6.tile_ref), custom_call_target="tpu_custom_call" | custom-call | flops 20000000000 | tf_op jit(solution)/shard_map/copies/pallas_call | solution.py:248
  25.2 0.0 copy-start
  25.2 8.8 %all-to-all-start = ((f32[16,48,128]{2,1,0:T(8,128)}), f32[16,48,128]{2,1,0:T(8,128)S(1)}, u32[]{:S(2)}, u32[]{:S(2)}) async-start(f32[16,48,128]{2,1,0:T(8,128)} %copies.1), calls=%async_computation | async-start | bytes 786432 | tf_op jit(solution)/shard_map/all_to_all | solution.py:258
  34.0 5.0 %collective-permute-start.2 = (bf16[768,128]{1,0:T(8,128)(2,1)S(1)}, bf16[768,128]{1,0:T(8,128)(2,1)S(1)}, u32[]{:S(2)}, u32[]{:S(2)}) collective-permute-start(bf16[768,128]{1,0:T(8,128)(2,1)S(1)} %relay.1.own_ref), channel_id=1, source_target_pairs={{0,2},{1,3},{2,0},{3,1},{4,6},{5,7},{6,4},{7,5},{8,10},{9,11},{10,... | collective-permute-start | bytes 589832 | tf_op jit(solution)/shard_map/ppermute | solution.py:207
  39.1 2.4 %collective-permute-start.3 = (bf16[768,128]{1,0:T(8,128)(2,1)S(1)}, bf16[768,128]{1,0:T(8,128)(2,1)S(1)}, u32[]{:S(2)}, u32[]{:S(2)}) collective-permute-start(bf16[768,128]{1,0:T(8,128)(2,1)S(1)} %relay.1.own_ref), channel_id=1, source_target_pairs={{0,6},{1,7},{2,4},{3,5},{4,2},{5,3},{6,0},{7,1},{8,14},{9,15},{10,... | collective-permute-start | bytes 589832 | tf_op jit(solution)/shard_map/ppermute | solution.py:207
  41.5 1.0 %collective-permute-done.2.first_ref = bf16[768,128]{1,0:T(8,128)(2,1)S(1)} collective-permute-done((bf16[768,128]{1,0:T(8,128)(2,1)S(1)}, bf16[768,128]{1,0:T(8,128)(2,1)S(1)}, u32[]{:S(2)}, u32[]{:S(2)}) %collective-permute-start.2) | collective-permute-done | bytes 196640 | tf_op jit(solution)/shard_map/ppermute | solution.py:207
  42.4 3.5 %collective-permute-start.4 = (bf16[768,128]{1,0:T(8,128)(2,1)S(1)}, bf16[768,128]{1,0:T(8,128)(2,1)S(1)}, u32[]{:S(2)}, u32[]{:S(2)}) collective-permute-start(bf16[768,128]{1,0:T(8,128)(2,1)S(1)} %collective-permute-done.2.first_ref), channel_id=1, source_target_pairs={{0,6},{1,7},{2,4},{3,5},{4,2},{5,3},{6,0},{7,1},{8,14},{9,15},{10,... | collective-permute-start | bytes 589832 | tf_op jit(solution)/shard_map/ppermute | solution.py:207
  45.9 1.1 %collective-permute-done.3.second_ref = bf16[768,128]{1,0:T(8,128)(2,1)S(1)} collective-permute-done((bf16[768,128]{1,0:T(8,128)(2,1)S(1)}, bf16[768,128]{1,0:T(8,128)(2,1)S(1)}, u32[]{:S(2)}, u32[]{:S(2)}) %collective-permute-start.3) | collective-permute-done | bytes 196640 | tf_op jit(solution)/shard_map/ppermute | solution.py:207
  47.0 0.1 pad_maximum_fusion
  47.1 6.7 %collective-permute-start.5 = (bf16[3,768,128]{2,1,0:T(8,128)(2,1)S(1)}, bf16[3,768,128]{2,1,0:T(8,128)(2,1)S(1)}, u32[]{:S(2)}, u32[]{:S(2)}) collective-permute-start(bf16[3,768,128]{2,1,0:T(8,128)(2,1)S(1)} %pad_maximum_fusion), channel_id=1, source_target_pairs={{0,1},{1,0},{2,3},{3,2},{4,5},{5,4},{6,7},{7,6},{8,9},{9,8},{10,11... | collective-permute-start | bytes 1769480 | tf_op jit(solution)/shard_map/ppermute | solution.py:207
  53.8 0.0 copy-start.1
  53.8 0.0 copy-start.2
  53.8 0.0 copy-start.3
  53.8 0.0 copy-start.4
  53.8 0.1 join.1
  53.9 2.5 %collective-permute-start.7 = (bf16[1920,128]{1,0:T(8,128)(2,1)S(1)}, bf16[1920,128]{1,0:T(8,128)(2,1)S(1)}, u32[]{:S(2)}, u32[]{:S(2)}) collective-permute-start(bf16[1920,128]{1,0:T(8,128)(2,1)S(1)} %get-tuple-element.11), channel_id=1, source_target_pairs={{0,1},{1,0},{2,3},{3,2},{4,5},{5,4},{6,7},{7,6},{8,9},{9,8},{10,11... | collective-permute-start | bytes 1474568 | tf_op jit(solution)/shard_map/ppermute | solution.py:207
  56.4 1.5 %collective-permute-done.7.theirs_b_ref = bf16[1920,128]{1,0:T(8,128)(2,1)S(1)} collective-permute-done((bf16[1920,128]{1,0:T(8,128)(2,1)S(1)}, bf16[1920,128]{1,0:T(8,128)(2,1)S(1)}, u32[]{:S(2)}, u32[]{:S(2)}) %collective-permute-start.7) | collective-permute-done | bytes 491552 | tf_op jit(solution)/shard_map/ppermute | solution.py:207
  57.9 3.8 %attend.1 = bf16[192,128]{1,0:T(8,128)(2,1)} custom-call(bf16[768,128]{1,0:T(8,128)(2,1)S(1)} %relay.1.own_ref, bf16[768,128]{1,0:T(8,128)(2,1)S(1)} %collective-permute-done.2.first_ref, bf16[768,128]{1,0:T(8,128)(2,1)S(1)} %collective-permute-done.3.second_ref, bf16[768,128]{1,0:T(8,128)(2,1)S(1)} %collective-permute-done.4.third_ref, ...), custom_call_target="tpu_custom_call" | custom-call | tf_op jit(solution)/shard_map/attend/pallas_call | solution.py:284
  (11 shorter events, 0.1 us)
Async XLA Ops:
  2.5 6.7 %collective-permute-start = (bf16[192,128]{1,0:T(8,128)(2,1)}, bf16[192,128]{1,0:T(8,128)(2,1)S(1)}, u32[]{:S(2)}, u32[]{:S(2)}) collective-permute-start(bf16[192,128]{1,0:T(8,128)(2,1)} %get-tuple-element.9.own_ref.nq_ref), channel_id=1, source_target_pairs={{0,8},{1,9},{2,10},{3,11},{4,12},{5,13},{6,14},{7,15},{8,0},{9,1},... | collective-permute-start | bytes 147464 | tf_op jit(solution)/shard_map/ppermute | solution.py:207
  7.6 16.7 %collective-permute-start.6 = (f32[48,128]{1,0:T(8,128)}, f32[48,128]{1,0:T(8,128)S(1)}, u32[]{:S(2)}, u32[]{:S(2)}) collective-permute-start(f32[48,128]{1,0:T(8,128)} %get-tuple-element.10), channel_id=1, source_target_pairs={{0,0},{1,1},{2,32},{3,33},{4,64},{5,65},{6,96},{7,97},{8,128},{9,1... | collective-permute-start | bytes 73736 | tf_op jit(solution)/shard_map/ppermute | solution.py:216
  10.1 23.9 %collective-permute-start.1 = (bf16[2,192,128]{2,1,0:T(8,128)(2,1)S(1)}, bf16[2,192,128]{2,1,0:T(8,128)(2,1)S(1)}, u32[]{:S(2)}, u32[]{:S(2)}) collective-permute-start(bf16[2,192,128]{2,1,0:T(8,128)(2,1)S(1)} %pad_maximum_fusion.1), channel_id=1, source_target_pairs={{0,24},{1,25},{2,26},{3,27},{4,28},{5,29},{6,30},{7,31},{8,16},{9,... | collective-permute-start | bytes 294920 | tf_op jit(solution)/shard_map/ppermute | solution.py:207
  25.2 8.8 %copy-start = (bf16[192,128]{1,0:T(8,128)(2,1)S(1)}, bf16[192,128]{1,0:T(8,128)(2,1)}, u32[]{:S(2)}) copy-start(bf16[192,128]{1,0:T(8,128)(2,1)} %get-tuple-element.9.own_ref.nq_ref) | copy-start | bytes 147460
  25.2 28.6 %all-to-all-start = ((f32[16,48,128]{2,1,0:T(8,128)}), f32[16,48,128]{2,1,0:T(8,128)S(1)}, u32[]{:S(2)}, u32[]{:S(2)}) async-start(f32[16,48,128]{2,1,0:T(8,128)} %copies.1), calls=%async_computation | async-start | bytes 786432 | tf_op jit(solution)/shard_map/all_to_all | solution.py:258
  34.0 8.4 %collective-permute-start.2 = (bf16[768,128]{1,0:T(8,128)(2,1)S(1)}, bf16[768,128]{1,0:T(8,128)(2,1)S(1)}, u32[]{:S(2)}, u32[]{:S(2)}) collective-permute-start(bf16[768,128]{1,0:T(8,128)(2,1)S(1)} %relay.1.own_ref), channel_id=1, source_target_pairs={{0,2},{1,3},{2,0},{3,1},{4,6},{5,7},{6,4},{7,5},{8,10},{9,11},{10,... | collective-permute-start | bytes 589832 | tf_op jit(solution)/shard_map/ppermute | solution.py:207
  39.1 7.9 %collective-permute-start.3 = (bf16[768,128]{1,0:T(8,128)(2,1)S(1)}, bf16[768,128]{1,0:T(8,128)(2,1)S(1)}, u32[]{:S(2)}, u32[]{:S(2)}) collective-permute-start(bf16[768,128]{1,0:T(8,128)(2,1)S(1)} %relay.1.own_ref), channel_id=1, source_target_pairs={{0,6},{1,7},{2,4},{3,5},{4,2},{5,3},{6,0},{7,1},{8,14},{9,15},{10,... | collective-permute-start | bytes 589832 | tf_op jit(solution)/shard_map/ppermute | solution.py:207
  42.4 11.3 %collective-permute-start.4 = (bf16[768,128]{1,0:T(8,128)(2,1)S(1)}, bf16[768,128]{1,0:T(8,128)(2,1)S(1)}, u32[]{:S(2)}, u32[]{:S(2)}) collective-permute-start(bf16[768,128]{1,0:T(8,128)(2,1)S(1)} %collective-permute-done.2.first_ref), channel_id=1, source_target_pairs={{0,6},{1,7},{2,4},{3,5},{4,2},{5,3},{6,0},{7,1},{8,14},{9,15},{10,... | collective-permute-start | bytes 589832 | tf_op jit(solution)/shard_map/ppermute | solution.py:207
  47.1 9.4 %collective-permute-start.5 = (bf16[3,768,128]{2,1,0:T(8,128)(2,1)S(1)}, bf16[3,768,128]{2,1,0:T(8,128)(2,1)S(1)}, u32[]{:S(2)}, u32[]{:S(2)}) collective-permute-start(bf16[3,768,128]{2,1,0:T(8,128)(2,1)S(1)} %pad_maximum_fusion), channel_id=1, source_target_pairs={{0,1},{1,0},{2,3},{3,2},{4,5},{5,4},{6,7},{7,6},{8,9},{9,8},{10,11... | collective-permute-start | bytes 1769480 | tf_op jit(solution)/shard_map/ppermute | solution.py:207
  53.8 4.1 %copy-start.1 = (bf16[128,256]{1,0:T(8,128)(2,1)S(1)}, bf16[128,256]{1,0:T(8,128)(2,1)}, u32[]{:S(2)}) copy-start(bf16[128,256]{1,0:T(8,128)(2,1)} %wkv_ref.1) | copy-start | bytes 196612
  53.8 4.1 %copy-start.2 = (bf16[128,128]{1,0:T(8,128)(2,1)S(1)}, bf16[128,128]{1,0:T(8,128)(2,1)}, u32[]{:S(2)}) copy-start(bf16[128,128]{1,0:T(8,128)(2,1)} %wq_ref.1) | copy-start | bytes 98308
  53.8 4.1 %copy-start.3 = (bf16[128,128]{1,0:T(8,128)(2,1)S(1)}, bf16[128,128]{1,0:T(8,128)(2,1)}, u32[]{:S(2)}) copy-start(bf16[128,128]{1,0:T(8,128)(2,1)} %wg_ref.1) | copy-start | bytes 98308
  53.8 4.1 %copy-start.4 = (bf16[128,128]{1,0:T(8,128)(2,1)S(1)}, bf16[128,128]{1,0:T(8,128)(2,1)}, u32[]{:S(2)}) copy-start(bf16[128,128]{1,0:T(8,128)(2,1)} %wo_ref.1) | copy-start | bytes 98308
  53.9 4.0 %collective-permute-start.7 = (bf16[1920,128]{1,0:T(8,128)(2,1)S(1)}, bf16[1920,128]{1,0:T(8,128)(2,1)S(1)}, u32[]{:S(2)}, u32[]{:S(2)}) collective-permute-start(bf16[1920,128]{1,0:T(8,128)(2,1)S(1)} %get-tuple-element.11), channel_id=1, source_target_pairs={{0,1},{1,0},{2,3},{3,2},{4,5},{5,4},{6,7},{7,6},{8,9},{9,8},{10,11... | collective-permute-start | bytes 1474568 | tf_op jit(solution)/shard_map/ppermute | solution.py:207

commit v3 on v1

--- a/solution.py
+++ b/solution.py
@@ -103,7 +103,7 @@
     y_hi = col // 8
     place = 0
     rest = []
-    for mask in MASKS:
+    for mask in (0, 1 + 2 * core, 3 - 2 * core, 2):
         for y_mask in MASKS:
             slot = lax.bitwise_xor(y_hi, y_mask) * 4 + lax.bitwise_xor(x, mask)
             mine = pl.multiple_of((slot * 2 + core) * KB, 8)
@@ -220,8 +220,8 @@
     return lambda c: c ^ (mask * 8)
 
 
-def near_x(mask):
-    return lambda c: c ^ (mask * 2)
+def ring_x(step):
+    return lambda c: c ^ (2 * ((1, 3)[(c + step) % 2]))
 
 
 def body(pair, ln_gain, w_query, w_keyval, w_gate, w_bias, w_out):
@@ -264,9 +264,9 @@
         cost_estimate=pl.CostEstimate(flops=30 * 10**9, bytes_accessed=0, transcendentals=0),
         name="relay",
     )(*ys)
-    first = permute_col(piece, near_x(1))
-    second = permute_col(piece, near_x(3))
-    third = permute_col(first, near_x(3))
+    first = permute_col(piece, ring_x(0))
+    second = permute_col(piece, ring_x(1))
+    third = permute_col(first, ring_x(1))
     mine = [piece, first, second, third]
     last, order = pl.pallas_call(
         join_kernel,

time: 60.7 us -> 61.9 us (1.020)
  waiting for transfers between devices: 2.21 us -> 4.57 us
  starting transfers between devices: 50 us -> 48.5 us
    ppermute x8, waiting for transfers between devices: 2.21 us -> 4.57 us  [permute_col(): return lax.ppermute(value, 'col', [(c, target(c)) for c in range(NCOL)])]
    ppermute x8, starting transfers between devices: 40.5 us -> 39 us  [permute_col(): return lax.ppermute(value, 'col', [(c, target(c)) for c in range(NCOL)])]
where the time goes in v3:
time: 61.9 us; the launch traced here: 60.7 us
  starting transfers between devices  48.5 us (78%)
  Pallas kernels  7.32 us (12%)
  waiting for transfers between devices  4.57 us (7%)
    ppermute x8, starting transfers between devices, permute_col(): return lax.ppermute(value, 'col', [(c, target(c)) for c in range(NCOL)])  39 us
    all_to_all x1, starting transfers between devices, body(): bias = lax.all_to_all(tiles, 'row', 0, 0)  8.09 us
    ppermute x8, waiting for transfers between devices, permute_col(): return lax.ppermute(value, 'col', [(c, target(c)) for c in range(NCOL)])  4.57 us
    pallas_call x1, Pallas kernels, body(): pl.pallas_call(attend_kernel, in_specs=[whole()] * 12, out_specs=whole(),...  3.79 us
    pallas_call x1, Pallas kernels, body(): pl.pallas_call(front_kernel, in_specs=[whole(pl.ANY)] * 3, out_specs=[who...  2.5 us
    ppermute x1, starting transfers between devices, permute_all(): return lax.ppermute(value, ('row', 'col'), pairs)  1.4 us
  transfers between devices with their start and end apart: 10, of which 3 were waited for; matrix products, arithmetic and copies ran while one was open for 0% of the time, Pallas kernels for 2%

profile of v3, /device:TPU:1, one launch (start us, length us, event | category | flops | bytes accessed | tf_op | source)
XLA Modules:
  0.0 60.7 jit_solution(8271892911978683542)
XLA Ops:
  0.0 2.5 %front.1 = (bf16[192,128]{1,0:T(8,128)(2,1)}, f32[48,128]{1,0:T(8,128)}) custom-call(bf16[1152,128]{1,0:T(8,128)(2,1)} %bitcast.12, f32[1,128]{1,0:T(1,128)} %bitcast.14, bf16[4,128]{1,0:T(4,128)(2,1)} %bitcast.13), custom_call_target="tpu_custom_call" | custom-call | tf_op jit(solution)/shard_map/front/pallas_call | solution.py:231
  2.5 1.4 %collective-permute-start.7 = (f32[48,128]{1,0:T(8,128)}, f32[48,128]{1,0:T(8,128)S(1)}, u32[]{:S(2)}, u32[]{:S(2)}) collective-permute-start(f32[48,128]{1,0:T(8,128)} %get-tuple-element.10), channel_id=1, source_target_pairs={{0,0},{1,1},{2,32},{3,33},{4,64},{5,65},{6,96},{7,97},{8,128},{9,1... | collective-permute-start | bytes 73736 | tf_op jit(solution)/shard_map/ppermute | solution.py:216
  3.9 9.2 %collective-permute-start = (bf16[192,128]{1,0:T(8,128)(2,1)}, bf16[192,128]{1,0:T(8,128)(2,1)S(1)}, u32[]{:S(2)}, u32[]{:S(2)}) collective-permute-start(bf16[192,128]{1,0:T(8,128)(2,1)} %get-tuple-element.9.own_ref.nq_ref), channel_id=1, source_target_pairs={{0,8},{1,9},{2,10},{3,11},{4,12},{5,13},{6,14},{7,15},{8,0},{9,1},... | collective-permute-start | bytes 147464 | tf_op jit(solution)/shard_map/ppermute | solution.py:207
  13.2 10.0 %collective-permute-start.1 = (bf16[192,128]{1,0:T(8,128)(2,1)}, bf16[192,128]{1,0:T(8,128)(2,1)S(1)}, u32[]{:S(2)}, u32[]{:S(2)}) collective-permute-start(bf16[192,128]{1,0:T(8,128)(2,1)} %get-tuple-element.9.own_ref.nq_ref), channel_id=1, source_target_pairs={{0,24},{1,25},{2,26},{3,27},{4,28},{5,29},{6,30},{7,31},{8,16},{9,... | collective-permute-start | bytes 147464 | tf_op jit(solution)/shard_map/ppermute | solution.py:207
  23.2 1.9 %collective-permute-start.2 = (bf16[192,128]{1,0:T(8,128)(2,1)}, bf16[192,128]{1,0:T(8,128)(2,1)S(1)}, u32[]{:S(2)}, u32[]{:S(2)}) collective-permute-start(bf16[192,128]{1,0:T(8,128)(2,1)} %get-tuple-element.9.own_ref.nq_ref), channel_id=1, source_target_pairs={{0,16},{1,17},{2,18},{3,19},{4,20},{5,21},{6,22},{7,23},{8,24},{9,... | collective-permute-start | bytes 147464 | tf_op jit(solution)/shard_map/ppermute | solution.py:207
  25.1 0.0 collective-permute-done.7.tile_ref
  25.1 0.9 %copies.1 = f32[16,48,128]{2,1,0:T(8,128)} custom-call(f32[48,128]{1,0:T(8,128)S(1)} %collective-permute-done.7.tile_ref), custom_call_target="tpu_custom_call" | custom-call | flops 20000000000 | tf_op jit(solution)/shard_map/copies/pallas_call | solution.py:247
  26.1 0.0 copy-start.1
  26.1 8.1 %all-to-all-start = ((f32[16,48,128]{2,1,0:T(8,128)}), f32[16,48,128]{2,1,0:T(8,128)S(1)}, u32[]{:S(2)}, u32[]{:S(2)}) async-start(f32[16,48,128]{2,1,0:T(8,128)} %copies.1), calls=%async_computation | async-start | bytes 786432 | tf_op jit(solution)/shard_map/all_to_all | solution.py:257
  34.2 4.0 %collective-permute-start.3 = (bf16[768,128]{1,0:T(8,128)(2,1)S(1)}, bf16[768,128]{1,0:T(8,128)(2,1)S(1)}, u32[]{:S(2)}, u32[]{:S(2)}) collective-permute-start(bf16[768,128]{1,0:T(8,128)(2,1)S(1)} %relay.1.own_ref), channel_id=1, source_target_pairs={{0,2},{1,7},{2,0},{3,5},{4,6},{5,3},{6,4},{7,1},{8,10},{9,15},{10,... | collective-permute-start | bytes 589832 | tf_op jit(solution)/shard_map/ppermute | solution.py:207
  38.3 1.9 %collective-permute-start.4 = (bf16[768,128]{1,0:T(8,128)(2,1)S(1)}, bf16[768,128]{1,0:T(8,128)(2,1)S(1)}, u32[]{:S(2)}, u32[]{:S(2)}) collective-permute-start(bf16[768,128]{1,0:T(8,128)(2,1)S(1)} %relay.1.own_ref), channel_id=1, source_target_pairs={{0,6},{1,3},{2,4},{3,1},{4,2},{5,7},{6,0},{7,5},{8,14},{9,11},{10,... | collective-permute-start | bytes 589832 | tf_op jit(solution)/shard_map/ppermute | solution.py:207
  40.2 2.0 %collective-permute-done.3.first_ref = bf16[768,128]{1,0:T(8,128)(2,1)S(1)} collective-permute-done((bf16[768,128]{1,0:T(8,128)(2,1)S(1)}, bf16[768,128]{1,0:T(8,128)(2,1)S(1)}, u32[]{:S(2)}, u32[]{:S(2)}) %collective-permute-start.3) | collective-permute-done | bytes 196640 | tf_op jit(solution)/shard_map/ppermute | solution.py:207
  42.2 2.0 %collective-permute-start.5 = (bf16[768,128]{1,0:T(8,128)(2,1)S(1)}, bf16[768,128]{1,0:T(8,128)(2,1)S(1)}, u32[]{:S(2)}, u32[]{:S(2)}) collective-permute-start(bf16[768,128]{1,0:T(8,128)(2,1)S(1)} %collective-permute-done.3.first_ref), channel_id=1, source_target_pairs={{0,6},{1,3},{2,4},{3,1},{4,2},{5,7},{6,0},{7,5},{8,14},{9,11},{10,... | collective-permute-start | bytes 589832 | tf_op jit(solution)/shard_map/ppermute | solution.py:207
  44.2 1.1 %collective-permute-done.4.second_ref = bf16[768,128]{1,0:T(8,128)(2,1)S(1)} collective-permute-done((bf16[768,128]{1,0:T(8,128)(2,1)S(1)}, bf16[768,128]{1,0:T(8,128)(2,1)S(1)}, u32[]{:S(2)}, u32[]{:S(2)}) %collective-permute-start.4) | collective-permute-done | bytes 196640 | tf_op jit(solution)/shard_map/ppermute | solution.py:207
  45.3 0.1 pad_maximum_fusion
  45.4 6.4 %collective-permute-start.6 = (bf16[3,768,128]{2,1,0:T(8,128)(2,1)S(1)}, bf16[3,768,128]{2,1,0:T(8,128)(2,1)S(1)}, u32[]{:S(2)}, u32[]{:S(2)}) collective-permute-start(bf16[3,768,128]{2,1,0:T(8,128)(2,1)S(1)} %pad_maximum_fusion), channel_id=1, source_target_pairs={{0,1},{1,0},{2,3},{3,2},{4,5},{5,4},{6,7},{7,6},{8,9},{9,8},{10,11... | collective-permute-start | bytes 1769480 | tf_op jit(solution)/shard_map/ppermute | solution.py:207
  51.8 0.0 copy-start
  51.8 0.0 copy-start.2
  51.8 0.0 copy-start.3
  51.8 0.0 copy-start.4
  51.9 0.1 join.1
  52.0 3.5 %collective-permute-start.8 = (bf16[1920,128]{1,0:T(8,128)(2,1)S(1)}, bf16[1920,128]{1,0:T(8,128)(2,1)S(1)}, u32[]{:S(2)}, u32[]{:S(2)}) collective-permute-start(bf16[1920,128]{1,0:T(8,128)(2,1)S(1)} %get-tuple-element.11), channel_id=1, source_target_pairs={{0,1},{1,0},{2,3},{3,2},{4,5},{5,4},{6,7},{7,6},{8,9},{9,8},{10,11... | collective-permute-start | bytes 1474568 | tf_op jit(solution)/shard_map/ppermute | solution.py:207
  55.5 1.5 %collective-permute-done.8.theirs_b_ref = bf16[1920,128]{1,0:T(8,128)(2,1)S(1)} collective-permute-done((bf16[1920,128]{1,0:T(8,128)(2,1)S(1)}, bf16[1920,128]{1,0:T(8,128)(2,1)S(1)}, u32[]{:S(2)}, u32[]{:S(2)}) %collective-permute-start.8) | collective-permute-done | bytes 491552 | tf_op jit(solution)/shard_map/ppermute | solution.py:207
  56.9 3.8 %attend.1 = bf16[192,128]{1,0:T(8,128)(2,1)} custom-call(bf16[768,128]{1,0:T(8,128)(2,1)S(1)} %relay.1.own_ref, bf16[768,128]{1,0:T(8,128)(2,1)S(1)} %collective-permute-done.3.first_ref, bf16[768,128]{1,0:T(8,128)(2,1)S(1)} %collective-permute-done.4.second_ref, bf16[768,128]{1,0:T(8,128)(2,1)S(1)} %collective-permute-done.5.third_ref, ...), custom_call_target="tpu_custom_call" | custom-call | tf_op jit(solution)/shard_map/attend/pallas_call | solution.py:283
  (12 shorter events, 0.1 us)
Async XLA Ops:
  2.5 22.6 %collective-permute-start.7 = (f32[48,128]{1,0:T(8,128)}, f32[48,128]{1,0:T(8,128)S(1)}, u32[]{:S(2)}, u32[]{:S(2)}) collective-permute-start(f32[48,128]{1,0:T(8,128)} %get-tuple-element.10), channel_id=1, source_target_pairs={{0,0},{1,1},{2,32},{3,33},{4,64},{5,65},{6,96},{7,97},{8,128},{9,1... | collective-permute-start | bytes 73736 | tf_op jit(solution)/shard_map/ppermute | solution.py:216
  3.9 30.3 %collective-permute-start = (bf16[192,128]{1,0:T(8,128)(2,1)}, bf16[192,128]{1,0:T(8,128)(2,1)S(1)}, u32[]{:S(2)}, u32[]{:S(2)}) collective-permute-start(bf16[192,128]{1,0:T(8,128)(2,1)} %get-tuple-element.9.own_ref.nq_ref), channel_id=1, source_target_pairs={{0,8},{1,9},{2,10},{3,11},{4,12},{5,13},{6,14},{7,15},{8,0},{9,1},... | collective-permute-start | bytes 147464 | tf_op jit(solution)/shard_map/ppermute | solution.py:207
  13.2 21.0 %collective-permute-start.1 = (bf16[192,128]{1,0:T(8,128)(2,1)}, bf16[192,128]{1,0:T(8,128)(2,1)S(1)}, u32[]{:S(2)}, u32[]{:S(2)}) collective-permute-start(bf16[192,128]{1,0:T(8,128)(2,1)} %get-tuple-element.9.own_ref.nq_ref), channel_id=1, source_target_pairs={{0,24},{1,25},{2,26},{3,27},{4,28},{5,29},{6,30},{7,31},{8,16},{9,... | collective-permute-start | bytes 147464 | tf_op jit(solution)/shard_map/ppermute | solution.py:207
  23.2 11.0 %collective-permute-start.2 = (bf16[192,128]{1,0:T(8,128)(2,1)}, bf16[192,128]{1,0:T(8,128)(2,1)S(1)}, u32[]{:S(2)}, u32[]{:S(2)}) collective-permute-start(bf16[192,128]{1,0:T(8,128)(2,1)} %get-tuple-element.9.own_ref.nq_ref), channel_id=1, source_target_pairs={{0,16},{1,17},{2,18},{3,19},{4,20},{5,21},{6,22},{7,23},{8,24},{9,... | collective-permute-start | bytes 147464 | tf_op jit(solution)/shard_map/ppermute | solution.py:207
  26.1 8.1 %copy-start.1 = (bf16[192,128]{1,0:T(8,128)(2,1)S(1)}, bf16[192,128]{1,0:T(8,128)(2,1)}, u32[]{:S(2)}) copy-start(bf16[192,128]{1,0:T(8,128)(2,1)} %get-tuple-element.9.own_ref.nq_ref) | copy-start | bytes 147460
  26.1 25.7 %all-to-all-start = ((f32[16,48,128]{2,1,0:T(8,128)}), f32[16,48,128]{2,1,0:T(8,128)S(1)}, u32[]{:S(2)}, u32[]{:S(2)}) async-start(f32[16,48,128]{2,1,0:T(8,128)} %copies.1), calls=%async_computation | async-start | bytes 786432 | tf_op jit(solution)/shard_map/all_to_all | solution.py:257
  34.2 7.9 %collective-permute-start.3 = (bf16[768,128]{1,0:T(8,128)(2,1)S(1)}, bf16[768,128]{1,0:T(8,128)(2,1)S(1)}, u32[]{:S(2)}, u32[]{:S(2)}) collective-permute-start(bf16[768,128]{1,0:T(8,128)(2,1)S(1)} %relay.1.own_ref), channel_id=1, source_target_pairs={{0,2},{1,7},{2,0},{3,5},{4,6},{5,3},{6,4},{7,1},{8,10},{9,15},{10,... | collective-permute-start | bytes 589832 | tf_op jit(solution)/shard_map/ppermute | solution.py:207
  38.3 7.0 %collective-permute-start.4 = (bf16[768,128]{1,0:T(8,128)(2,1)S(1)}, bf16[768,128]{1,0:T(8,128)(2,1)S(1)}, u32[]{:S(2)}, u32[]{:S(2)}) collective-permute-start(bf16[768,128]{1,0:T(8,128)(2,1)S(1)} %relay.1.own_ref), channel_id=1, source_target_pairs={{0,6},{1,3},{2,4},{3,1},{4,2},{5,7},{6,0},{7,5},{8,14},{9,11},{10,... | collective-permute-start | bytes 589832 | tf_op jit(solution)/shard_map/ppermute | solution.py:207
  42.2 9.6 %collective-permute-start.5 = (bf16[768,128]{1,0:T(8,128)(2,1)S(1)}, bf16[768,128]{1,0:T(8,128)(2,1)S(1)}, u32[]{:S(2)}, u32[]{:S(2)}) collective-permute-start(bf16[768,128]{1,0:T(8,128)(2,1)S(1)} %collective-permute-done.3.first_ref), channel_id=1, source_target_pairs={{0,6},{1,3},{2,4},{3,1},{4,2},{5,7},{6,0},{7,5},{8,14},{9,11},{10,... | collective-permute-start | bytes 589832 | tf_op jit(solution)/shard_map/ppermute | solution.py:207
  45.4 10.1 %collective-permute-start.6 = (bf16[3,768,128]{2,1,0:T(8,128)(2,1)S(1)}, bf16[3,768,128]{2,1,0:T(8,128)(2,1)S(1)}, u32[]{:S(2)}, u32[]{:S(2)}) collective-permute-start(bf16[3,768,128]{2,1,0:T(8,128)(2,1)S(1)} %pad_maximum_fusion), channel_id=1, source_target_pairs={{0,1},{1,0},{2,3},{3,2},{4,5},{5,4},{6,7},{7,6},{8,9},{9,8},{10,11... | collective-permute-start | bytes 1769480 | tf_op jit(solution)/shard_map/ppermute | solution.py:207
  51.8 5.1 %copy-start = (bf16[128,256]{1,0:T(8,128)(2,1)S(1)}, bf16[128,256]{1,0:T(8,128)(2,1)}, u32[]{:S(2)}) copy-start(bf16[128,256]{1,0:T(8,128)(2,1)} %wkv_ref.1) | copy-start | bytes 196612
  51.8 5.1 %copy-start.2 = (bf16[128,128]{1,0:T(8,128)(2,1)S(1)}, bf16[128,128]{1,0:T(8,128)(2,1)}, u32[]{:S(2)}) copy-start(bf16[128,128]{1,0:T(8,128)(2,1)} %wq_ref.1) | copy-start | bytes 98308
  51.8 5.1 %copy-start.3 = (bf16[128,128]{1,0:T(8,128)(2,1)S(1)}, bf16[128,128]{1,0:T(8,128)(2,1)}, u32[]{:S(2)}) copy-start(bf16[128,128]{1,0:T(8,128)(2,1)} %wg_ref.1) | copy-start | bytes 98308
  51.8 5.1 %copy-start.4 = (bf16[128,128]{1,0:T(8,128)(2,1)S(1)}, bf16[128,128]{1,0:T(8,128)(2,1)}, u32[]{:S(2)}) copy-start(bf16[128,128]{1,0:T(8,128)(2,1)} %wo_ref.1) | copy-start | bytes 98308
  52.0 5.0 %collective-permute-start.8 = (bf16[1920,128]{1,0:T(8,128)(2,1)S(1)}, bf16[1920,128]{1,0:T(8,128)(2,1)S(1)}, u32[]{:S(2)}, u32[]{:S(2)}) collective-permute-start(bf16[1920,128]{1,0:T(8,128)(2,1)S(1)} %get-tuple-element.11), channel_id=1, source_target_pairs={{0,1},{1,0},{2,3},{3,2},{4,5},{5,4},{6,7},{7,6},{8,9},{9,8},{10,11... | collective-permute-start | bytes 1474568 | tf_op jit(solution)/shard_map/ppermute | solution.py:207

commit v4 on v1

--- a/solution.py
+++ b/solution.py
@@ -266,7 +266,7 @@
     )(*ys)
     first = permute_col(piece, near_x(1))
     second = permute_col(piece, near_x(3))
-    third = permute_col(first, near_x(3))
+    third = permute_col(piece, near_x(2))
     mine = [piece, first, second, third]
     last, order = pl.pallas_call(
         join_kernel,

time: 60.7 us -> 63.1 us (1.040)
  waiting for transfers between devices: 2.21 us -> 3.94 us
  starting transfers between devices: 50 us -> 50.7 us
    ppermute x8, waiting for transfers between devices: 2.21 us -> 3.93 us  [permute_col(): return lax.ppermute(value, 'col', [(c, target(c)) for c in range(NCOL)])]
    ppermute x8, starting transfers between devices: 40.5 us -> 41.2 us  [permute_col(): return lax.ppermute(value, 'col', [(c, target(c)) for c in range(NCOL)])]
  transfers between devices with their start and end apart: 10 -> 10, of which waited for: 3 -> 2; matrix products, arithmetic and copies ran while one was open for 0% -> 0% of each run, Pallas kernels for 2% -> 2%
where the time goes in v4:
time: 63.1 us; the launch traced here: 62.3 us
  starting transfers between devices  50.7 us (80%)
  Pallas kernels  7.32 us (12%)
  waiting for transfers between devices  3.94 us (6%)
    ppermute x8, starting transfers between devices, permute_col(): return lax.ppermute(value, 'col', [(c, target(c)) for c in range(NCOL)])  41.2 us
    all_to_all x1, starting transfers between devices, body(): bias = lax.all_to_all(tiles, 'row', 0, 0)  8.09 us
    ppermute x8, waiting for transfers between devices, permute_col(): return lax.ppermute(value, 'col', [(c, target(c)) for c in range(NCOL)])  3.93 us
    pallas_call x1, Pallas kernels, body(): pl.pallas_call(attend_kernel, in_specs=[whole()] * 12, out_specs=whole(),...  3.79 us
    pallas_call x1, Pallas kernels, body(): pl.pallas_call(front_kernel, in_specs=[whole(pl.ANY)] * 3, out_specs=[who...  2.5 us
    ppermute x1, starting transfers between devices, permute_all(): return lax.ppermute(value, ('row', 'col'), pairs)  1.4 us
  transfers between devices with their start and end apart: 10, of which 2 were waited for; matrix products, arithmetic and copies ran while one was open for 0% of the time, Pallas kernels for 2%

profile of v4, /device:TPU:1, one launch (start us, length us, event | category | flops | bytes accessed | tf_op | source)
XLA Modules:
  0.0 62.3 jit_solution(566318493062403287)
XLA Ops:
  0.0 2.5 %front.1 = (bf16[192,128]{1,0:T(8,128)(2,1)}, f32[48,128]{1,0:T(8,128)}) custom-call(bf16[1152,128]{1,0:T(8,128)(2,1)} %bitcast.12, f32[1,128]{1,0:T(1,128)} %bitcast.14, bf16[4,128]{1,0:T(4,128)(2,1)} %bitcast.13), custom_call_target="tpu_custom_call" | custom-call | tf_op jit(solution)/shard_map/front/pallas_call | solution.py:231
  2.5 1.4 %collective-permute-start.7 = (f32[48,128]{1,0:T(8,128)}, f32[48,128]{1,0:T(8,128)S(1)}, u32[]{:S(2)}, u32[]{:S(2)}) collective-permute-start(f32[48,128]{1,0:T(8,128)} %get-tuple-element.10), channel_id=1, source_target_pairs={{0,0},{1,1},{2,32},{3,33},{4,64},{5,65},{6,96},{7,97},{8,128},{9,1... | collective-permute-start | bytes 73736 | tf_op jit(solution)/shard_map/ppermute | solution.py:216
  3.9 9.2 %collective-permute-start = (bf16[192,128]{1,0:T(8,128)(2,1)}, bf16[192,128]{1,0:T(8,128)(2,1)S(1)}, u32[]{:S(2)}, u32[]{:S(2)}) collective-permute-start(bf16[192,128]{1,0:T(8,128)(2,1)} %get-tuple-element.9.own_ref.nq_ref), channel_id=1, source_target_pairs={{0,8},{1,9},{2,10},{3,11},{4,12},{5,13},{6,14},{7,15},{8,0},{9,1},... | collective-permute-start | bytes 147464 | tf_op jit(solution)/shard_map/ppermute | solution.py:207
  13.2 10.0 %collective-permute-start.1 = (bf16[192,128]{1,0:T(8,128)(2,1)}, bf16[192,128]{1,0:T(8,128)(2,1)S(1)}, u32[]{:S(2)}, u32[]{:S(2)}) collective-permute-start(bf16[192,128]{1,0:T(8,128)(2,1)} %get-tuple-element.9.own_ref.nq_ref), channel_id=1, source_target_pairs={{0,24},{1,25},{2,26},{3,27},{4,28},{5,29},{6,30},{7,31},{8,16},{9,... | collective-permute-start | bytes 147464 | tf_op jit(solution)/shard_map/ppermute | solution.py:207
  23.2 1.9 %collective-permute-start.2 = (bf16[192,128]{1,0:T(8,128)(2,1)}, bf16[192,128]{1,0:T(8,128)(2,1)S(1)}, u32[]{:S(2)}, u32[]{:S(2)}) collective-permute-start(bf16[192,128]{1,0:T(8,128)(2,1)} %get-tuple-element.9.own_ref.nq_ref), channel_id=1, source_target_pairs={{0,16},{1,17},{2,18},{3,19},{4,20},{5,21},{6,22},{7,23},{8,24},{9,... | collective-permute-start | bytes 147464 | tf_op jit(solution)/shard_map/ppermute | solution.py:207
  25.1 0.0 collective-permute-done.7.tile_ref
  25.1 0.9 %copies.1 = f32[16,48,128]{2,1,0:T(8,128)} custom-call(f32[48,128]{1,0:T(8,128)S(1)} %collective-permute-done.7.tile_ref), custom_call_target="tpu_custom_call" | custom-call | flops 20000000000 | tf_op jit(solution)/shard_map/copies/pallas_call | solution.py:247
  26.1 0.0 copy-start.1
  26.1 8.1 %all-to-all-start = ((f32[16,48,128]{2,1,0:T(8,128)}), f32[16,48,128]{2,1,0:T(8,128)S(1)}, u32[]{:S(2)}, u32[]{:S(2)}) async-start(f32[16,48,128]{2,1,0:T(8,128)} %copies.1), calls=%async_computation | async-start | bytes 786432 | tf_op jit(solution)/shard_map/all_to_all | solution.py:257
  34.2 0.0 collective-permute-done.1.second_ref
  34.2 3.2 %collective-permute-start.3 = (bf16[768,128]{1,0:T(8,128)(2,1)S(1)}, bf16[768,128]{1,0:T(8,128)(2,1)S(1)}, u32[]{:S(2)}, u32[]{:S(2)}) collective-permute-start(bf16[768,128]{1,0:T(8,128)(2,1)S(1)} %relay.1.own_ref), channel_id=1, source_target_pairs={{0,2},{1,3},{2,0},{3,1},{4,6},{5,7},{6,4},{7,5},{8,10},{9,11},{10,... | collective-permute-start | bytes 589832 | tf_op jit(solution)/shard_map/ppermute | solution.py:207
  37.5 3.2 %collective-permute-start.4 = (bf16[768,128]{1,0:T(8,128)(2,1)S(1)}, bf16[768,128]{1,0:T(8,128)(2,1)S(1)}, u32[]{:S(2)}, u32[]{:S(2)}) collective-permute-start(bf16[768,128]{1,0:T(8,128)(2,1)S(1)} %relay.1.own_ref), channel_id=1, source_target_pairs={{0,6},{1,7},{2,4},{3,5},{4,2},{5,3},{6,0},{7,1},{8,14},{9,15},{10,... | collective-permute-start | bytes 589832 | tf_op jit(solution)/shard_map/ppermute | solution.py:207
  40.7 2.6 %collective-permute-start.5 = (bf16[768,128]{1,0:T(8,128)(2,1)S(1)}, bf16[768,128]{1,0:T(8,128)(2,1)S(1)}, u32[]{:S(2)}, u32[]{:S(2)}) collective-permute-start(bf16[768,128]{1,0:T(8,128)(2,1)S(1)} %relay.1.own_ref), channel_id=1, source_target_pairs={{0,4},{1,5},{2,6},{3,7},{4,0},{5,1},{6,2},{7,3},{8,12},{9,13},{10,... | collective-permute-start | bytes 589832 | tf_op jit(solution)/shard_map/ppermute | solution.py:207
  43.3 2.1 %collective-permute-done.4.second_ref = bf16[768,128]{1,0:T(8,128)(2,1)S(1)} collective-permute-done((bf16[768,128]{1,0:T(8,128)(2,1)S(1)}, bf16[768,128]{1,0:T(8,128)(2,1)S(1)}, u32[]{:S(2)}, u32[]{:S(2)}) %collective-permute-start.4) | collective-permute-done | bytes 196640 | tf_op jit(solution)/shard_map/ppermute | solution.py:207
  45.4 0.1 pad_maximum_fusion
  45.5 9.1 %collective-permute-start.6 = (bf16[3,768,128]{2,1,0:T(8,128)(2,1)S(1)}, bf16[3,768,128]{2,1,0:T(8,128)(2,1)S(1)}, u32[]{:S(2)}, u32[]{:S(2)}) collective-permute-start(bf16[3,768,128]{2,1,0:T(8,128)(2,1)S(1)} %pad_maximum_fusion), channel_id=1, source_target_pairs={{0,1},{1,0},{2,3},{3,2},{4,5},{5,4},{6,7},{7,6},{8,9},{9,8},{10,11... | collective-permute-start | bytes 1769480 | tf_op jit(solution)/shard_map/ppermute | solution.py:207
  54.6 0.0 copy-start
  54.6 0.0 copy-start.2
  54.6 0.0 copy-start.3
  54.6 0.0 copy-start.4
  54.6 0.1 join.1
  54.7 1.9 %collective-permute-start.8 = (bf16[1920,128]{1,0:T(8,128)(2,1)S(1)}, bf16[1920,128]{1,0:T(8,128)(2,1)S(1)}, u32[]{:S(2)}, u32[]{:S(2)}) collective-permute-start(bf16[1920,128]{1,0:T(8,128)(2,1)S(1)} %get-tuple-element.11), channel_id=1, source_target_pairs={{0,1},{1,0},{2,3},{3,2},{4,5},{5,4},{6,7},{7,6},{8,9},{9,8},{10,11... | collective-permute-start | bytes 1474568 | tf_op jit(solution)/shard_map/ppermute | solution.py:207
  56.7 1.8 %collective-permute-done.8.theirs_b_ref = bf16[1920,128]{1,0:T(8,128)(2,1)S(1)} collective-permute-done((bf16[1920,128]{1,0:T(8,128)(2,1)S(1)}, bf16[1920,128]{1,0:T(8,128)(2,1)S(1)}, u32[]{:S(2)}, u32[]{:S(2)}) %collective-permute-start.8) | collective-permute-done | bytes 491552 | tf_op jit(solution)/shard_map/ppermute | solution.py:207
  58.5 3.8 %attend.1 = bf16[192,128]{1,0:T(8,128)(2,1)} custom-call(bf16[768,128]{1,0:T(8,128)(2,1)S(1)} %relay.1.own_ref, bf16[768,128]{1,0:T(8,128)(2,1)S(1)} %collective-permute-done.3.first_ref, bf16[768,128]{1,0:T(8,128)(2,1)S(1)} %collective-permute-done.4.second_ref, bf16[768,128]{1,0:T(8,128)(2,1)S(1)} %collective-permute-done.5.third_ref, ...), custom_call_target="tpu_custom_call" | custom-call | tf_op jit(solution)/shard_map/attend/pallas_call | solution.py:283
  (12 shorter events, 0.1 us)
Async XLA Ops:
  2.5 22.6 %collective-permute-start.7 = (f32[48,128]{1,0:T(8,128)}, f32[48,128]{1,0:T(8,128)S(1)}, u32[]{:S(2)}, u32[]{:S(2)}) collective-permute-start(f32[48,128]{1,0:T(8,128)} %get-tuple-element.10), channel_id=1, source_target_pairs={{0,0},{1,1},{2,32},{3,33},{4,64},{5,65},{6,96},{7,97},{8,128},{9,1... | collective-permute-start | bytes 73736 | tf_op jit(solution)/shard_map/ppermute | solution.py:216
  3.9 30.3 %collective-permute-start = (bf16[192,128]{1,0:T(8,128)(2,1)}, bf16[192,128]{1,0:T(8,128)(2,1)S(1)}, u32[]{:S(2)}, u32[]{:S(2)}) collective-permute-start(bf16[192,128]{1,0:T(8,128)(2,1)} %get-tuple-element.9.own_ref.nq_ref), channel_id=1, source_target_pairs={{0,8},{1,9},{2,10},{3,11},{4,12},{5,13},{6,14},{7,15},{8,0},{9,1},... | collective-permute-start | bytes 147464 | tf_op jit(solution)/shard_map/ppermute | solution.py:207
  13.2 21.0 %collective-permute-start.1 = (bf16[192,128]{1,0:T(8,128)(2,1)}, bf16[192,128]{1,0:T(8,128)(2,1)S(1)}, u32[]{:S(2)}, u32[]{:S(2)}) collective-permute-start(bf16[192,128]{1,0:T(8,128)(2,1)} %get-tuple-element.9.own_ref.nq_ref), channel_id=1, source_target_pairs={{0,24},{1,25},{2,26},{3,27},{4,28},{5,29},{6,30},{7,31},{8,16},{9,... | collective-permute-start | bytes 147464 | tf_op jit(solution)/shard_map/ppermute | solution.py:207
  23.2 11.0 %collective-permute-start.2 = (bf16[192,128]{1,0:T(8,128)(2,1)}, bf16[192,128]{1,0:T(8,128)(2,1)S(1)}, u32[]{:S(2)}, u32[]{:S(2)}) collective-permute-start(bf16[192,128]{1,0:T(8,128)(2,1)} %get-tuple-element.9.own_ref.nq_ref), channel_id=1, source_target_pairs={{0,16},{1,17},{2,18},{3,19},{4,20},{5,21},{6,22},{7,23},{8,24},{9,... | collective-permute-start | bytes 147464 | tf_op jit(solution)/shard_map/ppermute | solution.py:207
  26.1 8.1 %copy-start.1 = (bf16[192,128]{1,0:T(8,128)(2,1)S(1)}, bf16[192,128]{1,0:T(8,128)(2,1)}, u32[]{:S(2)}) copy-start(bf16[192,128]{1,0:T(8,128)(2,1)} %get-tuple-element.9.own_ref.nq_ref) | copy-start | bytes 147460
  26.1 28.5 %all-to-all-start = ((f32[16,48,128]{2,1,0:T(8,128)}), f32[16,48,128]{2,1,0:T(8,128)S(1)}, u32[]{:S(2)}, u32[]{:S(2)}) async-start(f32[16,48,128]{2,1,0:T(8,128)} %copies.1), calls=%async_computation | async-start | bytes 786432 | tf_op jit(solution)/shard_map/all_to_all | solution.py:257
  34.2 9.1 %collective-permute-start.3 = (bf16[768,128]{1,0:T(8,128)(2,1)S(1)}, bf16[768,128]{1,0:T(8,128)(2,1)S(1)}, u32[]{:S(2)}, u32[]{:S(2)}) collective-permute-start(bf16[768,128]{1,0:T(8,128)(2,1)S(1)} %relay.1.own_ref), channel_id=1, source_target_pairs={{0,2},{1,3},{2,0},{3,1},{4,6},{5,7},{6,4},{7,5},{8,10},{9,11},{10,... | collective-permute-start | bytes 589832 | tf_op jit(solution)/shard_map/ppermute | solution.py:207
  37.5 7.9 %collective-permute-start.4 = (bf16[768,128]{1,0:T(8,128)(2,1)S(1)}, bf16[768,128]{1,0:T(8,128)(2,1)S(1)}, u32[]{:S(2)}, u32[]{:S(2)}) collective-permute-start(bf16[768,128]{1,0:T(8,128)(2,1)S(1)} %relay.1.own_ref), channel_id=1, source_target_pairs={{0,6},{1,7},{2,4},{3,5},{4,2},{5,3},{6,0},{7,1},{8,14},{9,15},{10,... | collective-permute-start | bytes 589832 | tf_op jit(solution)/shard_map/ppermute | solution.py:207
  40.7 13.9 %collective-permute-start.5 = (bf16[768,128]{1,0:T(8,128)(2,1)S(1)}, bf16[768,128]{1,0:T(8,128)(2,1)S(1)}, u32[]{:S(2)}, u32[]{:S(2)}) collective-permute-start(bf16[768,128]{1,0:T(8,128)(2,1)S(1)} %relay.1.own_ref), channel_id=1, source_target_pairs={{0,4},{1,5},{2,6},{3,7},{4,0},{5,1},{6,2},{7,3},{8,12},{9,13},{10,... | collective-permute-start | bytes 589832 | tf_op jit(solution)/shard_map/ppermute | solution.py:207
  45.5 11.2 %collective-permute-start.6 = (bf16[3,768,128]{2,1,0:T(8,128)(2,1)S(1)}, bf16[3,768,128]{2,1,0:T(8,128)(2,1)S(1)}, u32[]{:S(2)}, u32[]{:S(2)}) collective-permute-start(bf16[3,768,128]{2,1,0:T(8,128)(2,1)S(1)} %pad_maximum_fusion), channel_id=1, source_target_pairs={{0,1},{1,0},{2,3},{3,2},{4,5},{5,4},{6,7},{7,6},{8,9},{9,8},{10,11... | collective-permute-start | bytes 1769480 | tf_op jit(solution)/shard_map/ppermute | solution.py:207
  54.6 3.9 %copy-start = (bf16[128,256]{1,0:T(8,128)(2,1)S(1)}, bf16[128,256]{1,0:T(8,128)(2,1)}, u32[]{:S(2)}) copy-start(bf16[128,256]{1,0:T(8,128)(2,1)} %wkv_ref.1) | copy-start | bytes 196612
  54.6 3.9 %copy-start.2 = (bf16[128,128]{1,0:T(8,128)(2,1)S(1)}, bf16[128,128]{1,0:T(8,128)(2,1)}, u32[]{:S(2)}) copy-start(bf16[128,128]{1,0:T(8,128)(2,1)} %wq_ref.1) | copy-start | bytes 98308
  54.6 3.9 %copy-start.3 = (bf16[128,128]{1,0:T(8,128)(2,1)S(1)}, bf16[128,128]{1,0:T(8,128)(2,1)}, u32[]{:S(2)}) copy-start(bf16[128,128]{1,0:T(8,128)(2,1)} %wg_ref.1) | copy-start | bytes 98308
  54.6 3.9 %copy-start.4 = (bf16[128,128]{1,0:T(8,128)(2,1)S(1)}, bf16[128,128]{1,0:T(8,128)(2,1)}, u32[]{:S(2)}) copy-start(bf16[128,128]{1,0:T(8,128)(2,1)} %wo_ref.1) | copy-start | bytes 98308
  54.7 3.8 %collective-permute-start.8 = (bf16[1920,128]{1,0:T(8,128)(2,1)S(1)}, bf16[1920,128]{1,0:T(8,128)(2,1)S(1)}, u32[]{:S(2)}, u32[]{:S(2)}) collective-permute-start(bf16[1920,128]{1,0:T(8,128)(2,1)S(1)} %get-tuple-element.11), channel_id=1, source_target_pairs={{0,1},{1,0},{2,3},{3,2},{4,5},{5,4},{6,7},{7,6},{8,9},{9,8},{10,11... | collective-permute-start | bytes 1474568 | tf_op jit(solution)/shard_map/ppermute | solution.py:207

commit v5 on v1

--- a/solution.py
+++ b/solution.py
@@ -132,7 +132,7 @@
 def attend_kernel(
     own_ref, first_ref, second_ref, third_ref, theirs_a_ref, theirs_b_ref, order_ref,
     nq_ref, wq_ref, wkv_ref, wg_ref, wo_ref,
-    out_ref, bias_ref, held_ref, gate_ref, gated_ref,
+    out_ref, bias_ref, gate_ref, gated_ref,
 ):
     sources = (
         own_ref, first_ref, second_ref, third_ref,
@@ -181,9 +181,8 @@
         for n in range(2):
             a = 2 * i + n
             full = score[n * GROUP : (n + 1) * GROUP, :] + bias_ref[...]
-            held_ref[a % 4] = full
             top = jnp.max(full, axis=1, keepdims=True)
-            weights = jnp.exp(held_ref[a % 4] - top)
+            weights = jnp.exp(full - top)
             total = jnp.sum(weights, axis=1, keepdims=True)
             high = weights.astype(BF16)
             low = (weights - high.astype(F32)).astype(BF16)
@@ -192,7 +191,7 @@
                 values[:, n * LANES : (n + 1) * LANES],
                 preferred_element_type=F32,
             )
-            attended = (both[:GROUP, :] + both[GROUP:, :]) / total
+            attended = (both[:GROUP, :] + both[GROUP:, :]) * (1.0 / total)
             mine = jnp.zeros((KB, LANES), F32)
             for h in range(HEADS):
                 mine = jnp.where(lane // 32 == h, attended[h * KB : (h + 1) * KB, :], mine)
@@ -287,7 +286,6 @@
         out_shape=shape((nrows, LANES), BF16),
         scratch_shapes=[
             VM((GROUP, N_RES), F32),
-            VM((4, GROUP, N_RES), F32),
             VM((nrows, LANES), F32),
             VM((nrows, LANES), F32),
         ],

time: 60.7 us -> 60.7 us (level)
  no operation moved by 1% of the time
where the time goes in v5:
time: 60.7 us; the launch traced here: 59.9 us
  starting transfers between devices  50 us (82%)
  Pallas kernels  7.32 us (12%)
  waiting for transfers between devices  2.21 us (4%)
    ppermute x8, starting transfers between devices, permute_col(): return lax.ppermute(value, 'col', [(c, target(c)) for c in range(NCOL)])  40.5 us
    all_to_all x1, starting transfers between devices, body(): bias = lax.all_to_all(tiles, 'row', 0, 0)  8.09 us
    pallas_call x1, Pallas kernels, body(): pl.pallas_call(attend_kernel, in_specs=[whole()] * 12, out_specs=whole(),...  3.79 us
    pallas_call x1, Pallas kernels, body(): pl.pallas_call(front_kernel, in_specs=[whole(pl.ANY)] * 3, out_specs=[who...  2.5 us
    ppermute x8, waiting for transfers between devices, permute_col(): return lax.ppermute(value, 'col', [(c, target(c)) for c in range(NCOL)])  2.21 us
    ppermute x1, starting transfers between devices, permute_all(): return lax.ppermute(value, ('row', 'col'), pairs)  1.4 us
  transfers between devices with their start and end apart: 10, of which 3 were waited for; matrix products, arithmetic and copies ran while one was open for 0% of the time, Pallas kernels for 2%

profile of v5, /device:TPU:1, one launch (start us, length us, event | category | flops | bytes accessed | tf_op | source)
XLA Modules:
  0.0 59.9 jit_solution(2675463270500687109)
XLA Ops:
  0.0 2.5 %front.1 = (bf16[192,128]{1,0:T(8,128)(2,1)}, f32[48,128]{1,0:T(8,128)}) custom-call(bf16[1152,128]{1,0:T(8,128)(2,1)} %bitcast.12, f32[1,128]{1,0:T(1,128)} %bitcast.14, bf16[4,128]{1,0:T(4,128)(2,1)} %bitcast.13), custom_call_target="tpu_custom_call" | custom-call | tf_op jit(solution)/shard_map/front/pallas_call | solution.py:230
  2.5 1.4 %collective-permute-start.7 = (f32[48,128]{1,0:T(8,128)}, f32[48,128]{1,0:T(8,128)S(1)}, u32[]{:S(2)}, u32[]{:S(2)}) collective-permute-start(f32[48,128]{1,0:T(8,128)} %get-tuple-element.10), channel_id=1, source_target_pairs={{0,0},{1,1},{2,32},{3,33},{4,64},{5,65},{6,96},{7,97},{8,128},{9,1... | collective-permute-start | bytes 73736 | tf_op jit(solution)/shard_map/ppermute | solution.py:215
  3.9 9.2 %collective-permute-start = (bf16[192,128]{1,0:T(8,128)(2,1)}, bf16[192,128]{1,0:T(8,128)(2,1)S(1)}, u32[]{:S(2)}, u32[]{:S(2)}) collective-permute-start(bf16[192,128]{1,0:T(8,128)(2,1)} %get-tuple-element.9.own_ref.nq_ref), channel_id=1, source_target_pairs={{0,8},{1,9},{2,10},{3,11},{4,12},{5,13},{6,14},{7,15},{8,0},{9,1},... | collective-permute-start | bytes 147464 | tf_op jit(solution)/shard_map/ppermute | solution.py:206
  13.2 10.0 %collective-permute-start.1 = (bf16[192,128]{1,0:T(8,128)(2,1)}, bf16[192,128]{1,0:T(8,128)(2,1)S(1)}, u32[]{:S(2)}, u32[]{:S(2)}) collective-permute-start(bf16[192,128]{1,0:T(8,128)(2,1)} %get-tuple-element.9.own_ref.nq_ref), channel_id=1, source_target_pairs={{0,24},{1,25},{2,26},{3,27},{4,28},{5,29},{6,30},{7,31},{8,16},{9,... | collective-permute-start | bytes 147464 | tf_op jit(solution)/shard_map/ppermute | solution.py:206
  23.2 1.9 %collective-permute-start.2 = (bf16[192,128]{1,0:T(8,128)(2,1)}, bf16[192,128]{1,0:T(8,128)(2,1)S(1)}, u32[]{:S(2)}, u32[]{:S(2)}) collective-permute-start(bf16[192,128]{1,0:T(8,128)(2,1)} %get-tuple-element.9.own_ref.nq_ref), channel_id=1, source_target_pairs={{0,16},{1,17},{2,18},{3,19},{4,20},{5,21},{6,22},{7,23},{8,24},{9,... | collective-permute-start | bytes 147464 | tf_op jit(solution)/shard_map/ppermute | solution.py:206
  25.1 0.0 collective-permute-done.7.tile_ref
  25.1 0.9 %copies.1 = f32[16,48,128]{2,1,0:T(8,128)} custom-call(f32[48,128]{1,0:T(8,128)S(1)} %collective-permute-done.7.tile_ref), custom_call_target="tpu_custom_call" | custom-call | flops 20000000000 | tf_op jit(solution)/shard_map/copies/pallas_call | solution.py:246
  26.1 0.0 copy-start.1
  26.1 8.1 %all-to-all-start = ((f32[16,48,128]{2,1,0:T(8,128)}), f32[16,48,128]{2,1,0:T(8,128)S(1)}, u32[]{:S(2)}, u32[]{:S(2)}) async-start(f32[16,48,128]{2,1,0:T(8,128)} %copies.1), calls=%async_computation | async-start | bytes 786432 | tf_op jit(solution)/shard_map/all_to_all | solution.py:256
  34.2 3.2 %collective-permute-start.3 = (bf16[768,128]{1,0:T(8,128)(2,1)S(1)}, bf16[768,128]{1,0:T(8,128)(2,1)S(1)}, u32[]{:S(2)}, u32[]{:S(2)}) collective-permute-start(bf16[768,128]{1,0:T(8,128)(2,1)S(1)} %relay.1.own_ref), channel_id=1, source_target_pairs={{0,2},{1,3},{2,0},{3,1},{4,6},{5,7},{6,4},{7,5},{8,10},{9,11},{10,... | collective-permute-start | bytes 589832 | tf_op jit(solution)/shard_map/ppermute | solution.py:206
  37.5 3.2 %collective-permute-start.4 = (bf16[768,128]{1,0:T(8,128)(2,1)S(1)}, bf16[768,128]{1,0:T(8,128)(2,1)S(1)}, u32[]{:S(2)}, u32[]{:S(2)}) collective-permute-start(bf16[768,128]{1,0:T(8,128)(2,1)S(1)} %relay.1.own_ref), channel_id=1, source_target_pairs={{0,6},{1,7},{2,4},{3,5},{4,2},{5,3},{6,0},{7,1},{8,14},{9,15},{10,... | collective-permute-start | bytes 589832 | tf_op jit(solution)/shard_map/ppermute | solution.py:206
  40.7 0.3 collective-permute-done.3.first_ref
  41.0 4.0 %collective-permute-start.5 = (bf16[768,128]{1,0:T(8,128)(2,1)S(1)}, bf16[768,128]{1,0:T(8,128)(2,1)S(1)}, u32[]{:S(2)}, u32[]{:S(2)}) collective-permute-start(bf16[768,128]{1,0:T(8,128)(2,1)S(1)} %collective-permute-done.3.first_ref), channel_id=1, source_target_pairs={{0,6},{1,7},{2,4},{3,5},{4,2},{5,3},{6,0},{7,1},{8,14},{9,15},{10,... | collective-permute-start | bytes 589832 | tf_op jit(solution)/shard_map/ppermute | solution.py:206
  45.0 0.4 collective-permute-done.4.second_ref
  45.4 0.1 pad_maximum_fusion
  45.5 6.0 %collective-permute-start.6 = (bf16[3,768,128]{2,1,0:T(8,128)(2,1)S(1)}, bf16[3,768,128]{2,1,0:T(8,128)(2,1)S(1)}, u32[]{:S(2)}, u32[]{:S(2)}) collective-permute-start(bf16[3,768,128]{2,1,0:T(8,128)(2,1)S(1)} %pad_maximum_fusion), channel_id=1, source_target_pairs={{0,1},{1,0},{2,3},{3,2},{4,5},{5,4},{6,7},{7,6},{8,9},{9,8},{10,11... | collective-permute-start | bytes 1769480 | tf_op jit(solution)/shard_map/ppermute | solution.py:206
  51.5 0.0 copy-start
  51.6 0.0 copy-start.2
  51.6 0.0 copy-start.3
  51.6 0.0 copy-start.4
  51.6 0.1 join.1
  51.7 2.9 %collective-permute-start.8 = (bf16[1920,128]{1,0:T(8,128)(2,1)S(1)}, bf16[1920,128]{1,0:T(8,128)(2,1)S(1)}, u32[]{:S(2)}, u32[]{:S(2)}) collective-permute-start(bf16[1920,128]{1,0:T(8,128)(2,1)S(1)} %get-tuple-element.11), channel_id=1, source_target_pairs={{0,1},{1,0},{2,3},{3,2},{4,5},{5,4},{6,7},{7,6},{8,9},{9,8},{10,11... | collective-permute-start | bytes 1474568 | tf_op jit(solution)/shard_map/ppermute | solution.py:206
  54.6 1.5 %collective-permute-done.8.theirs_b_ref = bf16[1920,128]{1,0:T(8,128)(2,1)S(1)} collective-permute-done((bf16[1920,128]{1,0:T(8,128)(2,1)S(1)}, bf16[1920,128]{1,0:T(8,128)(2,1)S(1)}, u32[]{:S(2)}, u32[]{:S(2)}) %collective-permute-start.8) | collective-permute-done | bytes 491552 | tf_op jit(solution)/shard_map/ppermute | solution.py:206
  56.1 3.8 %attend.1 = bf16[192,128]{1,0:T(8,128)(2,1)} custom-call(bf16[768,128]{1,0:T(8,128)(2,1)S(1)} %relay.1.own_ref, bf16[768,128]{1,0:T(8,128)(2,1)S(1)} %collective-permute-done.3.first_ref, bf16[768,128]{1,0:T(8,128)(2,1)S(1)} %collective-permute-done.4.second_ref, bf16[768,128]{1,0:T(8,128)(2,1)S(1)} %collective-permute-done.5.third_ref, ...), custom_call_target="tpu_custom_call" | custom-call | tf_op jit(solution)/shard_map/attend/pallas_call | solution.py:282
  (12 shorter events, 0.1 us)
Async XLA Ops:
  2.5 22.6 %collective-permute-start.7 = (f32[48,128]{1,0:T(8,128)}, f32[48,128]{1,0:T(8,128)S(1)}, u32[]{:S(2)}, u32[]{:S(2)}) collective-permute-start(f32[48,128]{1,0:T(8,128)} %get-tuple-element.10), channel_id=1, source_target_pairs={{0,0},{1,1},{2,32},{3,33},{4,64},{5,65},{6,96},{7,97},{8,128},{9,1... | collective-permute-start | bytes 73736 | tf_op jit(solution)/shard_map/ppermute | solution.py:215
  3.9 30.3 %collective-permute-start = (bf16[192,128]{1,0:T(8,128)(2,1)}, bf16[192,128]{1,0:T(8,128)(2,1)S(1)}, u32[]{:S(2)}, u32[]{:S(2)}) collective-permute-start(bf16[192,128]{1,0:T(8,128)(2,1)} %get-tuple-element.9.own_ref.nq_ref), channel_id=1, source_target_pairs={{0,8},{1,9},{2,10},{3,11},{4,12},{5,13},{6,14},{7,15},{8,0},{9,1},... | collective-permute-start | bytes 147464 | tf_op jit(solution)/shard_map/ppermute | solution.py:206
  13.2 21.0 %collective-permute-start.1 = (bf16[192,128]{1,0:T(8,128)(2,1)}, bf16[192,128]{1,0:T(8,128)(2,1)S(1)}, u32[]{:S(2)}, u32[]{:S(2)}) collective-permute-start(bf16[192,128]{1,0:T(8,128)(2,1)} %get-tuple-element.9.own_ref.nq_ref), channel_id=1, source_target_pairs={{0,24},{1,25},{2,26},{3,27},{4,28},{5,29},{6,30},{7,31},{8,16},{9,... | collective-permute-start | bytes 147464 | tf_op jit(solution)/shard_map/ppermute | solution.py:206
  23.2 11.0 %collective-permute-start.2 = (bf16[192,128]{1,0:T(8,128)(2,1)}, bf16[192,128]{1,0:T(8,128)(2,1)S(1)}, u32[]{:S(2)}, u32[]{:S(2)}) collective-permute-start(bf16[192,128]{1,0:T(8,128)(2,1)} %get-tuple-element.9.own_ref.nq_ref), channel_id=1, source_target_pairs={{0,16},{1,17},{2,18},{3,19},{4,20},{5,21},{6,22},{7,23},{8,24},{9,... | collective-permute-start | bytes 147464 | tf_op jit(solution)/shard_map/ppermute | solution.py:206
  26.1 8.1 %copy-start.1 = (bf16[192,128]{1,0:T(8,128)(2,1)S(1)}, bf16[192,128]{1,0:T(8,128)(2,1)}, u32[]{:S(2)}) copy-start(bf16[192,128]{1,0:T(8,128)(2,1)} %get-tuple-element.9.own_ref.nq_ref) | copy-start | bytes 147460
  26.1 25.5 %all-to-all-start = ((f32[16,48,128]{2,1,0:T(8,128)}), f32[16,48,128]{2,1,0:T(8,128)S(1)}, u32[]{:S(2)}, u32[]{:S(2)}) async-start(f32[16,48,128]{2,1,0:T(8,128)} %copies.1), calls=%async_computation | async-start | bytes 786432 | tf_op jit(solution)/shard_map/all_to_all | solution.py:256
  34.2 6.7 %collective-permute-start.3 = (bf16[768,128]{1,0:T(8,128)(2,1)S(1)}, bf16[768,128]{1,0:T(8,128)(2,1)S(1)}, u32[]{:S(2)}, u32[]{:S(2)}) collective-permute-start(bf16[768,128]{1,0:T(8,128)(2,1)S(1)} %relay.1.own_ref), channel_id=1, source_target_pairs={{0,2},{1,3},{2,0},{3,1},{4,6},{5,7},{6,4},{7,5},{8,10},{9,11},{10,... | collective-permute-start | bytes 589832 | tf_op jit(solution)/shard_map/ppermute | solution.py:206
  37.5 7.9 %collective-permute-start.4 = (bf16[768,128]{1,0:T(8,128)(2,1)S(1)}, bf16[768,128]{1,0:T(8,128)(2,1)S(1)}, u32[]{:S(2)}, u32[]{:S(2)}) collective-permute-start(bf16[768,128]{1,0:T(8,128)(2,1)S(1)} %relay.1.own_ref), channel_id=1, source_target_pairs={{0,6},{1,7},{2,4},{3,5},{4,2},{5,3},{6,0},{7,1},{8,14},{9,15},{10,... | collective-permute-start | bytes 589832 | tf_op jit(solution)/shard_map/ppermute | solution.py:206
  41.0 10.6 %collective-permute-start.5 = (bf16[768,128]{1,0:T(8,128)(2,1)S(1)}, bf16[768,128]{1,0:T(8,128)(2,1)S(1)}, u32[]{:S(2)}, u32[]{:S(2)}) collective-permute-start(bf16[768,128]{1,0:T(8,128)(2,1)S(1)} %collective-permute-done.3.first_ref), channel_id=1, source_target_pairs={{0,6},{1,7},{2,4},{3,5},{4,2},{5,3},{6,0},{7,1},{8,14},{9,15},{10,... | collective-permute-start | bytes 589832 | tf_op jit(solution)/shard_map/ppermute | solution.py:206
  45.5 9.1 %collective-permute-start.6 = (bf16[3,768,128]{2,1,0:T(8,128)(2,1)S(1)}, bf16[3,768,128]{2,1,0:T(8,128)(2,1)S(1)}, u32[]{:S(2)}, u32[]{:S(2)}) collective-permute-start(bf16[3,768,128]{2,1,0:T(8,128)(2,1)S(1)} %pad_maximum_fusion), channel_id=1, source_target_pairs={{0,1},{1,0},{2,3},{3,2},{4,5},{5,4},{6,7},{7,6},{8,9},{9,8},{10,11... | collective-permute-start | bytes 1769480 | tf_op jit(solution)/shard_map/ppermute | solution.py:206
  51.5 4.5 %copy-start = (bf16[128,256]{1,0:T(8,128)(2,1)S(1)}, bf16[128,256]{1,0:T(8,128)(2,1)}, u32[]{:S(2)}) copy-start(bf16[128,256]{1,0:T(8,128)(2,1)} %wkv_ref.1) | copy-start | bytes 196612
  51.6 4.5 %copy-start.2 = (bf16[128,128]{1,0:T(8,128)(2,1)S(1)}, bf16[128,128]{1,0:T(8,128)(2,1)}, u32[]{:S(2)}) copy-start(bf16[128,128]{1,0:T(8,128)(2,1)} %wq_ref.1) | copy-start | bytes 98308
  51.6 4.5 %copy-start.3 = (bf16[128,128]{1,0:T(8,128)(2,1)S(1)}, bf16[128,128]{1,0:T(8,128)(2,1)}, u32[]{:S(2)}) copy-start(bf16[128,128]{1,0:T(8,128)(2,1)} %wg_ref.1) | copy-start | bytes 98308
  51.6 4.5 %copy-start.4 = (bf16[128,128]{1,0:T(8,128)(2,1)S(1)}, bf16[128,128]{1,0:T(8,128)(2,1)}, u32[]{:S(2)}) copy-start(bf16[128,128]{1,0:T(8,128)(2,1)} %wo_ref.1) | copy-start | bytes 98308
  51.7 4.4 %collective-permute-start.8 = (bf16[1920,128]{1,0:T(8,128)(2,1)S(1)}, bf16[1920,128]{1,0:T(8,128)(2,1)S(1)}, u32[]{:S(2)}, u32[]{:S(2)}) collective-permute-start(bf16[1920,128]{1,0:T(8,128)(2,1)S(1)} %get-tuple-element.11), channel_id=1, source_target_pairs={{0,1},{1,0},{2,3},{3,2},{4,5},{5,4},{6,7},{7,6},{8,9},{9,8},{10,11... | collective-permute-start | bytes 1474568 | tf_op jit(solution)/shard_map/ppermute | solution.py:206
